TPU v7x, 512 devices: a whole 4x8x8 slice. The times are simulated.
512 devices in a mesh: bins: 64 (over y, x, z_hi), lon: 8 (over z_lo, core).
Axes of the slice: x: 4, y: 8, z: 8 (z_hi: 2, z_lo: 4; z = z_hi * 4 + z_lo), core: 2. Of those that a mesh axis runs over, the one named last changes fastest.
Arguments:
- spectrum: float32 [1152, 512, 128], P('bins', 'lon'), may hold values from 0.05 to 2
- wind_speed: float32 [512, 128], P('lon'), may hold values from 2 to 20
- wind_dir: float32 [512, 128], P('lon'), may hold values from -3.140625 to 3.140625
- flags: int32 [512, 128], P('lon'), may hold values from 0 to 2
Outputs:
- spectrum_out: float32 [1152, 512, 128], P('bins', 'lon')
Inputs may be any that keep to these rules, and one draw needn't show every extreme that they name: `flags`: 0 marks land, 1 open sea, 2 sea ice.
All inputs are finite; a program needn't handle non-finite values.
Results may differ from a plain program's by a relative error of at most 0.0003.
Values sent between devices are 32-bit elements; how exact they have to be, the bound alone decides.
A program may use at most 64 MiB of HBM per device.

v0:
```python
import math

import jax
import jax.numpy as jnp
from jax import lax
from jax.sharding import PartitionSpec as P

NF = 32
ND = 36
STEPS = 2


wind_gain = 0.5
quad_gain = 0.3
break_gain = 0.3
ice_loss = 1.0
courant = 0.6


def padded_2(block, sides, width):
    for axis, dim in sides:
        count = lax.axis_size(axis)
        forward = [(i, i + 1) for i in range(count - 1)]
        forward.append((count - 1, 0))
        backward = [(target, source) for source, target in forward]
        low = lax.ppermute(
            lax.slice_in_dim(block, block.shape[dim] - width, None, axis=dim), axis, forward
        )
        high = lax.ppermute(lax.slice_in_dim(block, 0, width, axis=dim), axis, backward)
        block = jnp.concatenate([low, block, high], axis=dim)
    return block


def spectral_tables(index, nfreq, ndir):
    direction = (index // nfreq).astype(jnp.float32)
    level = (index % nfreq).astype(jnp.float32)
    theta = direction * (2.0 * math.pi / ndir)
    ratio = jnp.power(1.05, level - nfreq // 2)
    group = jnp.power(1.1, -level)
    return (theta, ratio, group, index % nfreq)


def courants(theta, group, rows):
    lines = jnp.arange(rows).astype(jnp.float32)
    coslat = jnp.cos((lines - rows / 2 + 0.5) * (0.25 * math.pi / 180.0))
    east = courant * group * jnp.cos(theta) / coslat
    north = courant * group * jnp.sin(theta)
    return (east, north)


def sources(field, upper, lower, spread, theta, ratio, speed, heading, kinds):
    forcing = wind_gain * (speed * 0.1) * ratio * jnp.maximum(jnp.cos(theta - heading), 0.0) * field
    quad = quad_gain * ratio * (field * field * (upper + lower) - 2.0 * field * upper * lower)
    damping = break_gain * ratio * ratio * spread
    grown = (field + forcing + quad) / (1.0 + damping)
    frozen = field / (1.0 + damping + ice_loss)
    return jnp.where(kinds == 1, grown, jnp.where(kinds == 2, frozen, 0.0))


def upwind(padded, axis, length):

    def cells(offset):
        return lax.slice_in_dim(padded, 3 + offset, 3 + offset + length, axis=axis)

    plus = (
        -2.0 * cells(-3)
        + 15.0 * cells(-2)
        - 60.0 * cells(-1)
        + 20.0 * cells(0)
        + 30.0 * cells(1)
        - 3.0 * cells(2)
    ) / 60.0
    minus = (
        3.0 * cells(-2)
        - 30.0 * cells(-1)
        - 20.0 * cells(0)
        + 60.0 * cells(1)
        - 15.0 * cells(2)
        + 2.0 * cells(3)
    ) / 60.0
    return (plus, minus)


def tendency(extended, east, north):
    width = extended.shape[1] - 6
    inner = extended[:, 3:-3, :]
    east_plus, east_minus = upwind(extended, 1, width)
    padded = jnp.pad(inner, ((0, 0), (0, 0), (3, 3)))
    north_plus, north_minus = upwind(padded, 2, inner.shape[2])
    return -(
        east * jnp.where(east >= 0.0, east_plus, east_minus)
        + north * jnp.where(north >= 0.0, north_plus, north_minus)
    )


def propagate(field, east, north):

    def rate(current):
        return tendency(padded_2(current, (("lon", 1),), 3), east, north)

    one = field + rate(field)
    two = 0.75 * field + 0.25 * (one + rate(one))
    return field / 3.0 + 2.0 / 3.0 * (two + rate(two))


def shards(spectrum, wind_speed, wind_dir, flags):
    bins_here, lon_here, rows = spectrum.shape
    groups = lax.axis_size("bins")
    total = bins_here * groups
    points = lon_here * rows // groups
    place = lax.axis_index("bins")
    local_index = place * bins_here + jnp.arange(bins_here, dtype=jnp.int32)
    theta, ratio, group, level = spectral_tables(local_index, NF, ND)
    column = (bins_here, 1, 1)
    theta_c = theta.reshape(column)
    east, north = courants(theta_c, group.reshape(column), rows)
    every = jnp.arange(total, dtype=jnp.int32)
    all_theta, all_ratio, all_group, all_level = spectral_tables(every, NF, ND)
    all_theta = all_theta.reshape(total, 1)
    all_ratio = all_ratio.reshape(total, 1)
    all_upper = (all_level + 2 < NF).reshape(total, 1)
    all_lower = (all_level >= 2).reshape(total, 1)
    start = place * points
    point_speed = lax.dynamic_slice_in_dim(wind_speed.reshape(-1), start, points)
    point_heading = lax.dynamic_slice_in_dim(wind_dir.reshape(-1), start, points)
    point_kinds = lax.dynamic_slice_in_dim(flags.reshape(-1), start, points)
    field = spectrum
    for step in range(STEPS):
        gathered = lax.all_to_all(field, "bins", split_axis=1, concat_axis=0, tiled=True)
        gathered = gathered.reshape(total, points)
        upper = jnp.where(all_upper, jnp.roll(gathered, -(NF + 2), axis=0), 0.0)
        lower = jnp.where(all_lower, jnp.roll(gathered, 3 * NF + 2, axis=0), 0.0)
        spread = jnp.sum(all_ratio * all_ratio * gathered * gathered, axis=0) / total
        updated = sources(
            gathered,
            upper,
            lower,
            spread,
            all_theta,
            all_ratio,
            point_speed,
            point_heading,
            point_kinds,
        )
        field = lax.all_to_all(
            updated.reshape(total, 1, points), "bins", split_axis=0, concat_axis=1, tiled=True
        )
        field = propagate(field, east, north)
        field = jnp.where(flags != 0, field, 0.0)
    return field


def solution(mesh):
    return jax.shard_map(
        shards,
        mesh=mesh,
        in_specs=(P("bins", "lon", None), P("lon", None), P("lon", None), P("lon", None)),
        out_specs=P("bins", "lon", None),
        check_vma=False,
    )
```

profile of v0, /device:TPU:1, one launch (start us, length us, event | category | flops | bytes accessed | tf_op | source)
XLA Modules:
  0.0 212.4 jit_solution(3888854700273307986)
XLA Ops:
  0.0 2.3 %copy.38 = f32[18,64,128]{2,0,1:T(8,128)} copy(f32[18,64,128]{2,1,0:T(8,128)} %param.4) | data formatting | bytes 1179648 | tf_op args[0]
  2.3 19.7 %all-to-all-start = ((f32[18,64,128]{2,0,1:T(8,128)}), f32[18,64,128]{2,0,1:T(8,128)S(1)}, u32[]{:S(2)}, u32[]{:S(2)}) async-start(f32[18,64,128]{2,0,1:T(8,128)} %copy.38), calls=%async_computation | async-start | bytes 1572864 | tf_op jit(solution)/shard_map/all_to_all | solution.py:129
  22.0 0.8 dynamic_slice.11
  22.8 0.8 dynamic-slice_multiply_fusion
  23.5 0.1 broadcast_compare_fusion.4
  23.7 22.9 %all-to-all-done = f32[18,64,128]{2,0,1:T(8,128)S(1)} async-done(((f32[18,64,128]{2,0,1:T(8,128)}), f32[18,64,128]{2,0,1:T(8,128)S(1)}, u32[]{:S(2)}, u32[]{:S(2)}) %all-to-all-start) | async-done | bytes 589856 | tf_op jit(solution)/shard_map/all_to_all | solution.py:129
  46.6 0.1 reshape.898
  46.7 0.6 reshape.895
  47.4 0.3 fusion
  47.7 4.3 %fusion.107 = f32[1152,1,128]{2,0,1:T(8,128)} fusion(f32[1152,1,128]{2,0,1:T(8,128)S(1)} %bitcast.75, f32[1054,1,128]{2,0,1:T(8,128)S(1)} %slice_bitcast_fusion.3, f32[98,1,128]{2,0,1:T(8,128)S(1)} %slice_bitcast_fusion.5, f32[34,1,128]{2,0,1:T(8,128)S(1)} %slice_bitcast_fusion.7, f32[1118,1,128]{2,0,1:T(8,128)S(1)} %slice_bitcast_fusion.1, ...), kind=kLoop, calls=%fused_computation.199 | loop fusion | flops 3833856 | bytes 2381824 | tf_op jit(solution)/shard_map/jit(_where)/select_n | solution.py:57
  52.0 7.7 %all-to-all-start.1 = ((f32[1152,1,128]{2,1,0:T(1,128)}), f32[1152,1,128]{2,1,0:T(1,128)S(1)}, u32[]{:S(2)}, u32[]{:S(2)}) async-start(f32[1152,1,128]{2,1,0:T(1,128)} %bitcast.11), calls=%async_computation.1 | async-start | bytes 1179648 | tf_op jit(solution)/shard_map/all_to_all | solution.py:145
  59.8 0.1 sine_multiply_fusion
  59.8 0.1 broadcast_compare_fusion.1
  59.9 0.1 broadcast_divide_fusion
  60.0 19.7 %all-to-all-done.1 = f32[1152,1,128]{2,1,0:T(1,128)S(1)} async-done(((f32[1152,1,128]{2,1,0:T(1,128)}), f32[1152,1,128]{2,1,0:T(1,128)S(1)}, u32[]{:S(2)}, u32[]{:S(2)}) %all-to-all-start.1) | async-done | bytes 589856 | tf_op jit(solution)/shard_map/all_to_all | solution.py:145
  79.7 0.1 copy.67
  79.8 6.1 %collective-permute-start.1 = (f32[18,3,128]{2,1,0:T(4,128)S(1)}, f32[18,3,128]{2,1,0:T(4,128)S(1)}, u32[]{:S(2)}, u32[]{:S(2)}) collective-permute-start(f32[18,3,128]{2,1,0:T(4,128)S(1)} %get-tuple-element.15), channel_id=1, source_target_pairs={{1,0},{2,1},{3,2},{4,3},{5,4},{6,5},{7,6},{0,7},{9,8},{10,9},{11,1... | collective-permute-start | bytes 82952 | tf_op jit(solution)/shard_map/ppermute | solution.py:29
  85.9 2.9 %collective-permute-start = (f32[18,3,128]{2,1,0:T(4,128)S(1)}, f32[18,3,128]{2,1,0:T(4,128)S(1)}, u32[]{:S(2)}, u32[]{:S(2)}) collective-permute-start(f32[18,3,128]{2,1,0:T(4,128)S(1)} %get-tuple-element.16), channel_id=1, source_target_pairs={{0,1},{1,2},{2,3},{3,4},{4,5},{5,6},{6,7},{7,0},{8,9},{9,10},{10,1... | collective-permute-start | bytes 82952 | tf_op jit(solution)/shard_map/ppermute | solution.py:26
  88.9 0.1 broadcast_compare_fusion.2
  88.9 1.0 collective-permute-done
  89.9 1.7 fusion.105
  91.7 5.0 %collective-permute-start.3 = (f32[18,3,128]{2,1,0:T(4,128)S(1)}, f32[18,3,128]{2,1,0:T(4,128)S(1)}, u32[]{:S(2)}, u32[]{:S(2)}) collective-permute-start(f32[18,3,128]{2,1,0:T(4,128)S(1)} %get-tuple-element.13), channel_id=1, source_target_pairs={{1,0},{2,1},{3,2},{4,3},{5,4},{6,5},{7,6},{0,7},{9,8},{10,9},{11,1... | collective-permute-start | bytes 82952 | tf_op jit(solution)/shard_map/ppermute | solution.py:29
  96.7 1.9 collective-permute-start.2
  98.6 1.2 collective-permute-done.2
  99.8 1.8 fusion.89
  101.6 4.1 %collective-permute-start.4 = (f32[18,3,128]{2,1,0:T(4,128)S(1)}, f32[18,3,128]{2,1,0:T(4,128)S(1)}, u32[]{:S(2)}, u32[]{:S(2)}) collective-permute-start(f32[18,3,128]{2,1,0:T(4,128)S(1)} %get-tuple-element.11), channel_id=1, source_target_pairs={{0,1},{1,2},{2,3},{3,4},{4,5},{5,6},{6,7},{7,0},{8,9},{9,10},{10,1... | collective-permute-start | bytes 82952 | tf_op jit(solution)/shard_map/ppermute | solution.py:26
  105.7 3.7 %collective-permute-start.5 = (f32[18,3,128]{2,1,0:T(4,128)S(1)}, f32[18,3,128]{2,1,0:T(4,128)S(1)}, u32[]{:S(2)}, u32[]{:S(2)}) collective-permute-start(f32[18,3,128]{2,1,0:T(4,128)S(1)} %get-tuple-element.12), channel_id=1, source_target_pairs={{1,0},{2,1},{3,2},{4,3},{5,4},{6,5},{7,6},{0,7},{9,8},{10,9},{11,1... | collective-permute-start | bytes 82952 | tf_op jit(solution)/shard_map/ppermute | solution.py:29
  109.5 1.5 collective-permute-done.5
  111.0 1.8 fusion.230
  112.8 0.4 copy.47
  113.1 28.1 %all_to_all.66 = f32[18,64,128]{2,0,1:T(8,128)S(1)} all-to-all(f32[18,64,128]{2,0,1:T(8,128)S(1)} %copy.47), channel_id=1, replica_groups=mesh['bins'=64,'lon'=8] {'bins'}, dimensions={1} | all-to-all | bytes 1179648 | tf_op jit(solution)/shard_map/all_to_all | solution.py:129
  141.3 0.6 reshape.899
  142.0 0.3 fusion.1
  142.3 3.5 %fusion.111 = f32[1152,1,128]{2,0,1:T(8,128)S(1)} fusion(f32[1152,1,128]{2,0,1:T(8,128)S(1)} %bitcast.74, f32[1054,1,128]{2,0,1:T(8,128)S(1)} %slice_bitcast_fusion.2, f32[98,1,128]{2,0,1:T(8,128)S(1)} %slice_bitcast_fusion.4, f32[34,1,128]{2,0,1:T(8,128)S(1)} %slice_bitcast_fusion.6, f32[1118,1,128]{2,0,1:T(8,128)S(1)} %slice_bitcast_fusion, ...), kind=kLoop, calls=%fused_computation.203 | loop fusion | flops 3833856 | bytes 2381824 | tf_op jit(solution)/shard_map/jit(_where)/select_n | solution.py:57
  145.8 25.4 %all_to_all.67 = f32[1152,1,128]{2,1,0:T(1,128)S(1)} all-to-all(f32[1152,1,128]{2,1,0:T(1,128)S(1)} %bitcast.73), channel_id=1, replica_groups=mesh['bins'=64,'lon'=8] {'bins'}, dimensions={0} | all-to-all | bytes 1179648 | tf_op jit(solution)/shard_map/all_to_all | solution.py:145
  171.2 0.1 copy.66
  171.3 8.7 %collective-permute-start.7 = (f32[18,3,128]{2,1,0:T(4,128)S(1)}, f32[18,3,128]{2,1,0:T(4,128)S(1)}, u32[]{:S(2)}, u32[]{:S(2)}) collective-permute-start(f32[18,3,128]{2,1,0:T(4,128)S(1)} %get-tuple-element.9), channel_id=1, source_target_pairs={{1,0},{2,1},{3,2},{4,3},{5,4},{6,5},{7,6},{0,7},{9,8},{10,9},{11,1... | collective-permute-start | bytes 82952 | tf_op jit(solution)/shard_map/ppermute | solution.py:29
  180.0 4.1 %collective-permute-start.6 = (f32[18,3,128]{2,1,0:T(4,128)S(1)}, f32[18,3,128]{2,1,0:T(4,128)S(1)}, u32[]{:S(2)}, u32[]{:S(2)}) collective-permute-start(f32[18,3,128]{2,1,0:T(4,128)S(1)} %get-tuple-element.10), channel_id=1, source_target_pairs={{0,1},{1,2},{2,3},{3,4},{4,5},{5,6},{6,7},{7,0},{8,9},{9,10},{10,1... | collective-permute-start | bytes 82952 | tf_op jit(solution)/shard_map/ppermute | solution.py:26
  184.2 3.3 %collective-permute-done.6 = f32[18,3,128]{2,1,0:T(4,128)S(1)} collective-permute-done((f32[18,3,128]{2,1,0:T(4,128)S(1)}, f32[18,3,128]{2,1,0:T(4,128)S(1)}, u32[]{:S(2)}, u32[]{:S(2)}) %collective-permute-start.6) | collective-permute-done | bytes 27680 | tf_op jit(solution)/shard_map/ppermute | solution.py:26
  187.5 1.7 fusion.53
  189.2 6.4 %collective-permute-start.9 = (f32[18,3,128]{2,1,0:T(4,128)S(1)}, f32[18,3,128]{2,1,0:T(4,128)S(1)}, u32[]{:S(2)}, u32[]{:S(2)}) collective-permute-start(f32[18,3,128]{2,1,0:T(4,128)S(1)} %get-tuple-element.7), channel_id=1, source_target_pairs={{1,0},{2,1},{3,2},{4,3},{5,4},{6,5},{7,6},{0,7},{9,8},{10,9},{11,1... | collective-permute-start | bytes 82952 | tf_op jit(solution)/shard_map/ppermute | solution.py:29
  195.6 1.9 collective-permute-start.8
  197.6 1.2 collective-permute-done.8
  198.7 1.8 fusion.37
  200.5 4.1 %collective-permute-start.10 = (f32[18,3,128]{2,1,0:T(4,128)S(1)}, f32[18,3,128]{2,1,0:T(4,128)S(1)}, u32[]{:S(2)}, u32[]{:S(2)}) collective-permute-start(f32[18,3,128]{2,1,0:T(4,128)S(1)} %get-tuple-element.5), channel_id=1, source_target_pairs={{0,1},{1,2},{2,3},{3,4},{4,5},{5,6},{6,7},{7,0},{8,9},{9,10},{10,1... | collective-permute-start | bytes 82952 | tf_op jit(solution)/shard_map/ppermute | solution.py:26
  204.6 3.7 %collective-permute-start.11 = (f32[18,3,128]{2,1,0:T(4,128)S(1)}, f32[18,3,128]{2,1,0:T(4,128)S(1)}, u32[]{:S(2)}, u32[]{:S(2)}) collective-permute-start(f32[18,3,128]{2,1,0:T(4,128)S(1)} %get-tuple-element.6), channel_id=1, source_target_pairs={{1,0},{2,1},{3,2},{4,3},{5,4},{6,5},{7,6},{0,7},{9,8},{10,9},{11,1... | collective-permute-start | bytes 82952 | tf_op jit(solution)/shard_map/ppermute | solution.py:29
  208.4 1.5 collective-permute-done.11
  209.9 2.5 %fusion.231 = f32[18,64,128]{2,1,0:T(8,128)} fusion(f32[18,64,128]{2,1,0:T(8,128)S(1)} %fusion.37, f32[18,3,128]{2,1,0:T(4,128)S(1)} %collective-permute-done.11, f32[18,3,128]{2,1,0:T(4,128)S(1)} %collective-permute-done.10, f32[18]{0:T(128)S(1)} %get-tuple-element.25, f32[18,128]{1,0:T(8,128)S(1)} %broadcast_divide_fusion, ...), kind=kLoop, calls=%fused_computation.354 | loop fusion | flops 9142272 | bytes 1844570 | tf_op jit(solution)/shard_map/jit(_where)/select_n | solution.py:149
  (31 shorter events, 0.5 us)
Async XLA Ops:
  2.3 21.2 %copy-start = (s32[64,128]{1,0:T(8,128)S(1)}, s32[64,128]{1,0:T(8,128)}, u32[]{:S(2)}) copy-start(s32[64,128]{1,0:T(8,128)} %param.7) | copy-start | bytes 98308
  2.3 44.3 %all-to-all-start = ((f32[18,64,128]{2,0,1:T(8,128)}), f32[18,64,128]{2,0,1:T(8,128)S(1)}, u32[]{:S(2)}, u32[]{:S(2)}) async-start(f32[18,64,128]{2,0,1:T(8,128)} %copy.38), calls=%async_computation | async-start | bytes 1572864 | tf_op jit(solution)/shard_map/all_to_all | solution.py:129
  52.0 27.7 %all-to-all-start.1 = ((f32[1152,1,128]{2,1,0:T(1,128)}), f32[1152,1,128]{2,1,0:T(1,128)S(1)}, u32[]{:S(2)}, u32[]{:S(2)}) async-start(f32[1152,1,128]{2,1,0:T(1,128)} %bitcast.11), calls=%async_computation.1 | async-start | bytes 1179648 | tf_op jit(solution)/shard_map/all_to_all | solution.py:145
  79.8 9.1 %collective-permute-start.1 = (f32[18,3,128]{2,1,0:T(4,128)S(1)}, f32[18,3,128]{2,1,0:T(4,128)S(1)}, u32[]{:S(2)}, u32[]{:S(2)}) collective-permute-start(f32[18,3,128]{2,1,0:T(4,128)S(1)} %get-tuple-element.15), channel_id=1, source_target_pairs={{1,0},{2,1},{3,2},{4,3},{5,4},{6,5},{7,6},{0,7},{9,8},{10,9},{11,1... | collective-permute-start | bytes 82952 | tf_op jit(solution)/shard_map/ppermute | solution.py:29
  85.9 4.0 %collective-permute-start = (f32[18,3,128]{2,1,0:T(4,128)S(1)}, f32[18,3,128]{2,1,0:T(4,128)S(1)}, u32[]{:S(2)}, u32[]{:S(2)}) collective-permute-start(f32[18,3,128]{2,1,0:T(4,128)S(1)} %get-tuple-element.16), channel_id=1, source_target_pairs={{0,1},{1,2},{2,3},{3,4},{4,5},{5,6},{6,7},{7,0},{8,9},{9,10},{10,1... | collective-permute-start | bytes 82952 | tf_op jit(solution)/shard_map/ppermute | solution.py:26
  91.7 7.0 %collective-permute-start.3 = (f32[18,3,128]{2,1,0:T(4,128)S(1)}, f32[18,3,128]{2,1,0:T(4,128)S(1)}, u32[]{:S(2)}, u32[]{:S(2)}) collective-permute-start(f32[18,3,128]{2,1,0:T(4,128)S(1)} %get-tuple-element.13), channel_id=1, source_target_pairs={{1,0},{2,1},{3,2},{4,3},{5,4},{6,5},{7,6},{0,7},{9,8},{10,9},{11,1... | collective-permute-start | bytes 82952 | tf_op jit(solution)/shard_map/ppermute | solution.py:29
  96.7 3.1 %collective-permute-start.2 = (f32[18,3,128]{2,1,0:T(4,128)S(1)}, f32[18,3,128]{2,1,0:T(4,128)S(1)}, u32[]{:S(2)}, u32[]{:S(2)}) collective-permute-start(f32[18,3,128]{2,1,0:T(4,128)S(1)} %get-tuple-element.14), channel_id=1, source_target_pairs={{0,1},{1,2},{2,3},{3,4},{4,5},{5,6},{6,7},{7,0},{8,9},{9,10},{10,1... | collective-permute-start | bytes 82952 | tf_op jit(solution)/shard_map/ppermute | solution.py:26
  101.6 7.8 %collective-permute-start.4 = (f32[18,3,128]{2,1,0:T(4,128)S(1)}, f32[18,3,128]{2,1,0:T(4,128)S(1)}, u32[]{:S(2)}, u32[]{:S(2)}) collective-permute-start(f32[18,3,128]{2,1,0:T(4,128)S(1)} %get-tuple-element.11), channel_id=1, source_target_pairs={{0,1},{1,2},{2,3},{3,4},{4,5},{5,6},{6,7},{7,0},{8,9},{9,10},{10,1... | collective-permute-start | bytes 82952 | tf_op jit(solution)/shard_map/ppermute | solution.py:26
  105.7 5.3 %collective-permute-start.5 = (f32[18,3,128]{2,1,0:T(4,128)S(1)}, f32[18,3,128]{2,1,0:T(4,128)S(1)}, u32[]{:S(2)}, u32[]{:S(2)}) collective-permute-start(f32[18,3,128]{2,1,0:T(4,128)S(1)} %get-tuple-element.12), channel_id=1, source_target_pairs={{1,0},{2,1},{3,2},{4,3},{5,4},{6,5},{7,6},{0,7},{9,8},{10,9},{11,1... | collective-permute-start | bytes 82952 | tf_op jit(solution)/shard_map/ppermute | solution.py:29
  171.3 12.8 %collective-permute-start.7 = (f32[18,3,128]{2,1,0:T(4,128)S(1)}, f32[18,3,128]{2,1,0:T(4,128)S(1)}, u32[]{:S(2)}, u32[]{:S(2)}) collective-permute-start(f32[18,3,128]{2,1,0:T(4,128)S(1)} %get-tuple-element.9), channel_id=1, source_target_pairs={{1,0},{2,1},{3,2},{4,3},{5,4},{6,5},{7,6},{0,7},{9,8},{10,9},{11,1... | collective-permute-start | bytes 82952 | tf_op jit(solution)/shard_map/ppermute | solution.py:29
  180.0 7.5 %collective-permute-start.6 = (f32[18,3,128]{2,1,0:T(4,128)S(1)}, f32[18,3,128]{2,1,0:T(4,128)S(1)}, u32[]{:S(2)}, u32[]{:S(2)}) collective-permute-start(f32[18,3,128]{2,1,0:T(4,128)S(1)} %get-tuple-element.10), channel_id=1, source_target_pairs={{0,1},{1,2},{2,3},{3,4},{4,5},{5,6},{6,7},{7,0},{8,9},{9,10},{10,1... | collective-permute-start | bytes 82952 | tf_op jit(solution)/shard_map/ppermute | solution.py:26
  189.2 8.3 %collective-permute-start.9 = (f32[18,3,128]{2,1,0:T(4,128)S(1)}, f32[18,3,128]{2,1,0:T(4,128)S(1)}, u32[]{:S(2)}, u32[]{:S(2)}) collective-permute-start(f32[18,3,128]{2,1,0:T(4,128)S(1)} %get-tuple-element.7), channel_id=1, source_target_pairs={{1,0},{2,1},{3,2},{4,3},{5,4},{6,5},{7,6},{0,7},{9,8},{10,9},{11,1... | collective-permute-start | bytes 82952 | tf_op jit(solution)/shard_map/ppermute | solution.py:29
  195.6 3.1 %collective-permute-start.8 = (f32[18,3,128]{2,1,0:T(4,128)S(1)}, f32[18,3,128]{2,1,0:T(4,128)S(1)}, u32[]{:S(2)}, u32[]{:S(2)}) collective-permute-start(f32[18,3,128]{2,1,0:T(4,128)S(1)} %get-tuple-element.8), channel_id=1, source_target_pairs={{0,1},{1,2},{2,3},{3,4},{4,5},{5,6},{6,7},{7,0},{8,9},{9,10},{10,1... | collective-permute-start | bytes 82952 | tf_op jit(solution)/shard_map/ppermute | solution.py:26
  200.5 7.8 %collective-permute-start.10 = (f32[18,3,128]{2,1,0:T(4,128)S(1)}, f32[18,3,128]{2,1,0:T(4,128)S(1)}, u32[]{:S(2)}, u32[]{:S(2)}) collective-permute-start(f32[18,3,128]{2,1,0:T(4,128)S(1)} %get-tuple-element.5), channel_id=1, source_target_pairs={{0,1},{1,2},{2,3},{3,4},{4,5},{5,6},{6,7},{7,0},{8,9},{9,10},{10,1... | collective-permute-start | bytes 82952 | tf_op jit(solution)/shard_map/ppermute | solution.py:26
  204.6 5.3 %collective-permute-start.11 = (f32[18,3,128]{2,1,0:T(4,128)S(1)}, f32[18,3,128]{2,1,0:T(4,128)S(1)}, u32[]{:S(2)}, u32[]{:S(2)}) collective-permute-start(f32[18,3,128]{2,1,0:T(4,128)S(1)} %get-tuple-element.6), channel_id=1, source_target_pairs={{1,0},{2,1},{3,2},{4,3},{5,4},{6,5},{7,6},{0,7},{9,8},{10,9},{11,1... | collective-permute-start | bytes 82952 | tf_op jit(solution)/shard_map/ppermute | solution.py:29
where the time goes:
time: 215 us; the launch traced here: 212 us
  starting transfers between devices  80.1 us (37%)
  blocking collectives  53.5 us (25%)
  waiting for transfers between devices  52.4 us (24%)
  other arithmetic  20.8 us (10%)
  local copies, waits for them, and re-layouts  5.08 us (2%)
    ppermute x6, starting transfers between devices, padded_2(): lax.ppermute(lax.slice_in_dim(block, 0, width, axis=dim), axis, backward)  33.6 us
    all_to_all x1, blocking collectives, shards(): lax.all_to_all(field, 'bins', split_axis=1, concat_axis=0, tiled=True)  28.1 us
    all_to_all x1, blocking collectives, shards(): lax.all_to_all(updated.reshape(total, 1, points), 'bins', split_axis=0, c...  25.4 us
    all_to_all x1, waiting for transfers between devices, shards(): lax.all_to_all(field, 'bins', split_axis=1, concat_axis=0, tiled=True)  22.9 us
    all_to_all x1, waiting for transfers between devices, shards(): lax.all_to_all(updated.reshape(total, 1, points), 'bins', split_axis=0, c...  19.7 us
    all_to_all x1, starting transfers between devices, shards(): lax.all_to_all(field, 'bins', split_axis=1, concat_axis=0, tiled=True)  19.7 us
    ppermute x6, starting transfers between devices, padded_2(): lax.ppermute(lax.slice_in_dim(block, block.shape[dim] - width, None, axis...  19.1 us
    select_n x2, other arithmetic, sources(): return jnp.where(kinds == 1, grown, jnp.where(kinds == 2, frozen, 0.0))  7.78 us
  transfers between devices with their start and end apart: 14, of which 8 were waited for; matrix products, arithmetic and copies ran while one was open for 1% of the time, Pallas kernels for 0%

commit v1 on v0

v1 whole, which is shorter than its diff:
```python
import functools
import math

import jax
import jax.numpy as jnp
from jax import lax
from jax.experimental import pallas as pl
from jax.experimental.pallas import tpu as pltpu
from jax.sharding import PartitionSpec as P

NF = 32
ND = 36
STEPS = 2

wind_gain = 0.5
quad_gain = 0.3
break_gain = 0.3
ice_loss = 1.0
courant = 0.6

RING = 8
HALO = 9
BASE = 16
GROUP = 3
GROUPS = 6
LAG = 2
LEG = 2
PLUS = (-2.0, 15.0, -60.0, 20.0, 30.0, -3.0, 0.0)
MINUS = (0.0, 3.0, -30.0, -20.0, 60.0, -15.0, 2.0)

DIRECT = (
    (0, 0, 3, 2, -2), (0, 3, 3, 5, -2), (0, 6, 3, 8, -2), (0, 9, 3, 11, -2), (0, 12, 3, 14, -2), (0, 15, 1, 17, -2),
    (1, 16, 2, 6, 6),
)
SHARED = ((3, 12, 2, 0), (4, 14, 3, 2), (5, 17, 1, 5))
FAR = ((0, 16, 2, 0, -1), (1, 0, 3, 8, 1), (1, 3, 3, 11, -1), (1, 6, 3, 14, 1), (1, 9, 1, 17, -1))
KEPT_BACK = (1, 2)
S0, F0 = len(DIRECT), len(DIRECT) + len(SHARED)
PIECES = F0 + len(FAR)
NEEDS = (
    ((F0, 0, S0, S0 + 1), (1, S0 + 2), (2, 6, F0 + 1), (F0 + 2,), (F0 + 3,), (F0 + 4,)),
    ((F0, S0), (0, 1, S0 + 1, S0 + 2), (2, 6, F0 + 1), (F0 + 2,), (F0 + 3,), (F0 + 4,)),
)
FIRST_GROUP = (0, 1)

RATIO, COS, SIN, DAMP, UPPER, LOWER, EAST, WEST, NORTH, SOUTH = range(10)


def bin_table(index):
    direction = (index // NF).astype(jnp.float32)
    level = (index % NF).astype(jnp.float32)
    theta = direction * (2.0 * math.pi / ND)
    ratio = jnp.power(1.05, level - NF // 2)
    group = jnp.power(1.1, -level)
    east = courant * group * jnp.cos(theta)
    north = courant * group * jnp.sin(theta)
    ratio, theta, east, north, level = (v[:, None] for v in (ratio, theta, east, north, level))
    return jnp.concatenate(
        [
            ratio,
            jnp.cos(theta),
            jnp.sin(theta),
            break_gain * ratio * ratio / (NF * ND),
            (level + 2 < NF).astype(jnp.float32),
            (level >= 2).astype(jnp.float32),
            jnp.where(east >= 0.0, east / -60.0, 0.0),
            jnp.where(east >= 0.0, 0.0, east / -60.0),
            jnp.where(north >= 0.0, north / -60.0, 0.0),
            jnp.where(north >= 0.0, 0.0, north / -60.0),
        ],
        axis=1,
    )


def row_table(rows):
    lines = jnp.arange(rows)
    coslat = jnp.cos((lines.astype(jnp.float32) - rows / 2 + 0.5) * (0.25 * math.pi / 180.0))
    masks = [((lines + j >= 0) & (lines + j < rows)).astype(jnp.float32) for j in range(-3, 4)]
    return jnp.stack([1.0 / coslat] + masks, axis=0)


def kernel(
    field_hbm, speed_hbm, heading_hbm, flags_hbm, bins_ref, rows_ref, out_ref,
    first, later, last, got, relay, wide, one, two, speed, heading, flags, gain_x, gain_y, open_sea, ice,
    part, part_in, mid, mid_in, total,
    send_sem, got_sem, leg_send, leg_recv, halo_send, halo_recv,
    a_send, a_recv, b_send, b_recv, c_send, c_recv, in_sem, out_sem,
):
    here, columns, rows = field_hbm.shape
    count, sectors = lax.axis_size("bins"), lax.axis_size("lon")
    place, sector = lax.axis_index("bins"), lax.axis_index("lon")
    line, spot = place // RING, place % RING
    chunk = columns // RING
    def in_row(turn):
        return line * RING + (spot + turn) % RING

    def in_column(turn):
        return (line + turn) % RING * RING + spot

    def across(offset):
        return (place + offset + count) % count

    pair, far, core = place // 2, place % 2, sector % 2
    height = far * (sectors // 2) + sector // 2
    around_z = sectors

    def at(pair_offset, climb):
        new = (height + climb + around_z) % around_z
        new_pair = (pair + pair_offset + count // 2) % (count // 2)
        return {"bins": new_pair * 2 + new // (sectors // 2), "lon": new % (sectors // 2) * 2 + core}

    barrier = pltpu.get_barrier_semaphore()
    partners = [{"bins": across(s * o)} for o in (2, 6, 8) for s in (1, -1)]
    partners += [at(o, s * LEG) for o in (-3, -1, 0, 1, 3) for s in (1, -1)]
    partners += [{"bins": in_row(t)} for t in range(1, RING)]
    partners += [{"bins": in_column(t)} for t in range(1, RING)]
    partners += [{"lon": (sector + s + sectors) % sectors} for s in (1, -1)]
    for partner in partners:
        pl.semaphore_signal(barrier, inc=1, device_id=partner, device_id_type=pl.DeviceIdType.MESH)

    def send(src, dst, send_sem, recv_sem, device):
        return pltpu.make_async_remote_copy(
            src_ref=src, dst_ref=dst, send_sem=send_sem, recv_sem=recv_sem,
            device_id=device, device_id_type=pl.DeviceIdType.MESH,
        )

    def source_of(step):
        return field_hbm if step == 0 else later

    def field_of(step):
        return first if step == 0 else later

    def direct(step, piece):
        kind, b, bins, slot, places = DIRECT[piece]
        return send(
            source_of(step).at[pl.ds(b, bins)], got.at[step, kind, pl.ds(slot, bins)],
            send_sem.at[step, piece], got_sem.at[step, piece], {"bins": across(places)},
        )

    def shared(step, piece):
        _, slot, bins, new_slot = SHARED[piece]
        return send(
            got.at[step, 0, pl.ds(slot, bins)], got.at[step, 1, pl.ds(new_slot, bins)],
            send_sem.at[step, S0 + piece], got_sem.at[step, S0 + piece], {"bins": across(8)},
        )

    def leg(step, piece):
        kind, b, bins, _, way = FAR[piece]
        offset = 1 + 2 * far if kind else far - 1
        return send(
            source_of(step).at[pl.ds(b, bins)], relay.at[step, pl.ds(b, bins)],
            leg_send.at[step, piece], leg_recv.at[step, piece], at(offset, way * LEG),
        )

    def second_leg(step, piece):
        kind, b, bins, slot, way = FAR[piece]
        source_far = (height - way * LEG + around_z) % around_z // (sectors // 2)
        return send(
            relay.at[step, pl.ds(b, bins)], got.at[step, kind, pl.ds(slot, bins)],
            send_sem.at[step, F0 + piece], got_sem.at[step, F0 + piece], at(1 - source_far if kind else 0, way * LEG),
        )

    def arrival(step, piece):
        if piece < S0:
            return direct(step, piece)
        if piece < F0:
            return shared(step, piece - S0)
        return second_leg(step, piece - F0)

    def pass_on_far(step, pieces):
        for piece in pieces:
            leg(step, piece).wait_recv()
            second_leg(step, piece).start()

    def pass_on_shared(step):
        for piece, (before, *_) in enumerate(SHARED):
            direct(step, before).wait_recv()
            shared(step, piece).start()

    def halo_copy(step, group, side):
        if side == 0:
            src, dst, turn = BASE + columns - HALO, BASE - HALO, 1
        else:
            src, dst, turn = BASE, BASE + columns, -1
        ext = wide.at[step, pl.ds(group * GROUP, GROUP)]
        return send(
            ext.at[:, pl.ds(src, HALO)], ext.at[:, pl.ds(dst, HALO)],
            halo_send.at[step, side, group], halo_recv.at[step, side, group],
            {"lon": (sector + turn + sectors) % sectors},
        )

    def a_copy(step, turn):
        start = pl.multiple_of((spot + turn) % RING * chunk, chunk)
        return send(part.at[step, pl.ds(start, chunk)], part_in.at[step, turn], a_send.at[step, turn], a_recv.at[step, turn], {"bins": in_row(turn)})

    def b_copy(step, turn):
        return send(mid.at[step], mid_in.at[step, turn], b_send.at[step, turn], b_recv.at[step, turn], {"bins": in_column(turn)})

    def c_copy(step, turn):
        start = pl.multiple_of(spot * chunk, chunk)
        mine = total.at[step, pl.ds(start, chunk)]
        return send(mine, mine, c_send.at[step, turn], c_recv.at[step, turn], {"bins": in_row(turn)})

    def c_from(step, turn):
        start = pl.multiple_of((spot + RING - turn) % RING * chunk, chunk)
        theirs = total.at[step, pl.ds(start, chunk)]
        return send(theirs, theirs, c_send.at[step, turn], c_recv.at[step, turn], {"bins": in_row(turn)})

    def square(b, values):
        scaled = bins_ref[b, RATIO] * values
        return scaled * scaled

    def spread_a(step):
        for turn in range(1, RING):
            a_copy(step, turn).start()

    def spread_b(step):
        start = pl.multiple_of(spot * chunk, chunk)
        so_far = part[step, pl.ds(start, chunk)]
        for turn in range(1, RING):
            a_copy(step, turn).wait_recv()
            so_far += part_in[step, turn]
        mid[step] = so_far
        for turn in range(1, RING):
            b_copy(step, turn).start()

    def spread_c(step):
        start = pl.multiple_of(spot * chunk, chunk)
        so_far = mid[step]
        for turn in range(1, RING):
            b_copy(step, turn).wait_recv()
            so_far += mid_in[step, turn]
        total[step, pl.ds(start, chunk)] = so_far
        for turn in range(1, RING):
            c_copy(step, turn).start()

    def spread_end(step):
        for turn in range(1, RING):
            c_from(step, turn).wait_recv()

    def source(step, b):
        energy = field_of(step)[b]
        above = got[step, 0, b] * bins_ref[b, UPPER]
        below = got[step, 1, b] * bins_ref[b, LOWER]
        ratio = bins_ref[b, RATIO]
        wind = jnp.maximum(bins_ref[b, COS] * gain_x[...] + bins_ref[b, SIN] * gain_y[...], 0.0)
        quad = quad_gain * (energy * (above + below) - 2.0 * above * below)
        grown = energy + energy * (ratio * (wind + quad))
        top = jnp.where(open_sea[...] > 0.0, grown, energy)
        bottom = 1.0 + bins_ref[b, DAMP] * total[step] + ice[...]
        wide[step, b, pl.ds(BASE, columns)] = jnp.where(flags[...] == 0, 0.0, top / bottom)

    def rate(ref, start, length, lon, lat):
        centre = ref[pl.ds(start, length)]
        result = centre * (1.0 + lon[3] + lat[3])
        for j in (-3, -2, -1, 1, 2, 3):
            result += ref[pl.ds(start + j, length)] * lon[j + 3]
            result += pltpu.roll(centre, (-j) % rows, 1) * lat[j + 3]
        return result

    def advance(step, b, slot):
        lon = [(PLUS[j] * bins_ref[b, EAST] + MINUS[j] * bins_ref[b, WEST]) * rows_ref[0:1] for j in range(7)]
        lat = [(PLUS[j] * bins_ref[b, NORTH] + MINUS[j] * bins_ref[b, SOUTH]) * rows_ref[1 + j : 2 + j] for j in range(7)]
        ext, one_b, two_b = wide.at[step, b], one.at[slot], two.at[slot]
        around, wider = pl.ds(BASE - 8, columns + 16), columns + 16
        one_b[around] = rate(ext, BASE - 8, wider, lon, lat)
        two_b[around] = 0.75 * ext[around] + 0.25 * rate(one_b, BASE - 8, wider, lon, lat)
        moved = ext[pl.ds(BASE, columns)] / 3.0 + (2.0 / 3.0) * rate(two_b, BASE, columns, lon, lat)
        moved = jnp.where(flags[...] == 0, 0.0, moved)
        if step < STEPS - 1:
            later[b] = moved
            part[step + 1] += square(b, moved)
        else:
            last[b] = moved

    def result_copy(group):
        some = pl.ds(group * GROUP, GROUP)
        return pltpu.make_async_copy(last.at[some], out_ref.at[some], out_sem.at[group])

    def send_group(step, group):
        for k in range(GROUPS):
            @pl.when(group == k)
            def _(k=k):
                mine = range(k * GROUP, (k + 1) * GROUP)
                for piece, (_, b, *_) in enumerate(FAR):
                    if b in mine:
                        leg(step, piece).start()
                for piece, (_, b, *_) in enumerate(DIRECT):
                    if b in mine and piece not in KEPT_BACK:
                        direct(step, piece).start()

    inputs = [(field_hbm, first), (speed_hbm, speed), (heading_hbm, heading), (flags_hbm, flags)]
    inputs = [pltpu.make_async_copy(src, dst, in_sem.at[i]) for i, (src, dst) in enumerate(inputs)]
    for copy in inputs:
        copy.start()
    for step in range(1, STEPS):
        part[step] = jnp.zeros((columns, rows), jnp.float32)
    inputs[0].wait()
    part[0] = lax.fori_loop(0, here, lambda b, so_far: so_far + square(b, first[b]), jnp.zeros((columns, rows), jnp.float32))
    pl.semaphore_wait(barrier, len(partners))

    spread_a(0)
    for piece in range(len(FAR)):
        leg(0, piece).start()
    for piece in (3, 4, 5, 6, 0):
        direct(0, piece).start()
    for copy in inputs[1:]:
        copy.wait()
    gain = wind_gain * 0.1 * speed[...]
    gain_x[...] = gain * jnp.cos(heading[...])
    gain_y[...] = gain * jnp.sin(heading[...])
    open_sea[...] = jnp.where(flags[...] == 1, 1.0, 0.0)
    ice[...] = jnp.where(flags[...] == 2, ice_loss, 0.0)
    spread_b(0)
    direct(0, 1).start()
    pass_on_far(0, (0, 1, 2))
    spread_c(0)
    direct(0, 2).start()
    pass_on_far(0, (3, 4))
    pass_on_shared(0)
    spread_end(0)

    for step in range(STEPS):
        if step > 0:
            spread_a(step)
            direct(step, 1).start()
            pass_on_far(step, (1, 2))
            spread_b(step)
            direct(step, 2).start()
            pass_on_far(step, (3, 4))
            pass_on_shared(step)
            spread_c(step)
            pass_on_far(step, (0,))
            spread_end(step)

        @pl.loop(0, GROUPS + LAG)
        def _(g, step=step):
            @pl.when(g < GROUPS)
            def _():
                group = (g + FIRST_GROUP[step]) % GROUPS
                for k in range(GROUPS):
                    @pl.when(group == k)
                    def _(k=k):
                        for piece in NEEDS[step][k]:
                            arrival(step, piece).wait_recv()

                for j in range(GROUP):
                    source(step, group * GROUP + j)
                for side in range(2):
                    halo_copy(step, group, side).start()

            @pl.when(g >= LAG)
            def _():
                group = (g - LAG + FIRST_GROUP[step]) % GROUPS
                for side in range(2):
                    halo_copy(step, group, side).wait_recv()
                for j in range(GROUP):
                    advance(step, group * GROUP + j, j)
                if step < STEPS - 1:
                    send_group(step + 1, group)
                else:
                    result_copy(group).start()

    for step in range(STEPS):
        for turn in range(1, RING):
            a_copy(step, turn).wait_send()
            b_copy(step, turn).wait_send()
            c_copy(step, turn).wait_send()
        for piece in range(PIECES):
            arrival(step, piece).wait_send()
        for piece in range(len(FAR)):
            leg(step, piece).wait_send()

        @pl.loop(0, GROUPS)
        def _(group, step=step):
            for side in range(2):
                halo_copy(step, group, side).wait_send()

    @pl.loop(0, GROUPS)
    def _(group):
        result_copy(group).wait()


def shards(spectrum, wind_speed, wind_dir, flags):
    here, columns, rows = spectrum.shape
    index = lax.axis_index("bins") * here + jnp.arange(here, dtype=jnp.int32)
    whole = (columns, rows)
    chunk = columns // RING
    ext = columns + 2 * BASE
    hbm = pl.BlockSpec(memory_space=pl.ANY)
    dma = pltpu.SemaphoreType.DMA

    def buffer(*shape):
        return pltpu.VMEM(shape, jnp.float32)

    return pl.pallas_call(
        kernel,
        out_shape=jax.ShapeDtypeStruct(spectrum.shape, jnp.float32),
        in_specs=[hbm] * 4 + [pl.BlockSpec(memory_space=pltpu.SMEM), pl.BlockSpec(memory_space=pltpu.VMEM)],
        out_specs=hbm,
        scratch_shapes=[
            buffer(here, *whole),
            buffer(here, *whole),
            buffer(here, *whole),
            buffer(STEPS, 2, here, *whole),
            buffer(STEPS, here, *whole),
            buffer(STEPS, here, ext, rows),
            buffer(GROUP, ext, rows),
            buffer(GROUP, ext, rows),
            buffer(*whole),
            buffer(*whole),
            pltpu.VMEM(whole, jnp.int32),
            buffer(*whole),
            buffer(*whole),
            buffer(*whole),
            buffer(*whole),
            buffer(STEPS, *whole),
            buffer(STEPS, RING, chunk, rows),
            buffer(STEPS, chunk, rows),
            buffer(STEPS, RING, chunk, rows),
            buffer(STEPS, *whole),
        ]
        + [dma((STEPS, PIECES))] * 2
        + [dma((STEPS, len(FAR)))] * 2
        + [dma((STEPS, 2, GROUPS))] * 2
        + [dma((STEPS, RING))] * 6
        + [dma((4,)), dma((GROUPS,))],
        compiler_params=pltpu.CompilerParams(
            collective_id=0, has_side_effects=True, vmem_limit_bytes=24 * 1024 * 1024
        ),
    )(spectrum, wind_speed, wind_dir, flags, bin_table(index), row_table(rows))


def solution(mesh):
    return jax.shard_map(
        shards,
        mesh=mesh,
        in_specs=(P("bins", "lon", None), P("lon", None), P("lon", None), P("lon", None)),
        out_specs=P("bins", "lon", None),
        check_vma=False,
    )
```

time: 215 us -> 92.8 us (0.43); the launches traced: 212 us -> 92.6 us
  Pallas kernels: 0 us -> 89.5 us
  starting transfers between devices: 80.1 us -> 0 us
  blocking collectives: 53.5 us -> 0 us
  waiting for transfers between devices: 52.4 us -> 0 us
  other arithmetic: 20.8 us -> 0.34 us
  local copies, waits for them, and re-layouts: 5.08 us -> 2.68 us
    pallas_call x0 -> x1, Pallas kernels: none -> 89.5 us  [shards(): pl.pallas_call(kernel, out_shape=jax.ShapeDtypeStruct(spectrum.shape, jnp...]
    all_to_all x2 -> x0, blocking collectives: 53.5 us -> none  [the longest x1 28.1 us: shards(): lax.all_to_all(field, 'bins', split_axis=1, concat_axis=0, tiled=True)]
    ppermute x12 -> x0, starting transfers between devices: 52.7 us -> none  [the longest x6 33.6 us: padded_2(): lax.ppermute(lax.slice_in_dim(block, 0, width, axis=dim), axis, backward)]
    all_to_all x2 -> x0, waiting for transfers between devices: 42.7 us -> none  [the longest x1 22.9 us: shards(): lax.all_to_all(field, 'bins', split_axis=1, concat_axis=0, tiled=True)]
    all_to_all x2 -> x0, starting transfers between devices: 27.4 us -> none  [the longest x1 19.7 us: shards(): lax.all_to_all(field, 'bins', split_axis=1, concat_axis=0, tiled=True)]
    select_n x4 -> x2, other arithmetic: 12.1 us -> 0.16 us  [the longest x1 0.08 us: bin_table(): jnp.where(east >= 0.0, 0.0, east / -60.0)]
    ppermute x12 -> x0, waiting for transfers between devices: 9.71 us -> none  [the longest x6 6.64 us: padded_2(): lax.ppermute(lax.slice_in_dim(block, block.shape[dim] - width, None, axis...]
    add x4 -> x0, other arithmetic: 6.98 us -> none  [the longest x2 3.53 us: propagate(): two = 0.75 * field + 0.25 * (one + rate(one))]
  transfers between devices with their start and end apart: 14 -> 0, of which waited for: 8 -> 0; matrix products, arithmetic and copies ran while one was open for 1% -> 0% of each run, Pallas kernels for 0% -> 0%
where the time goes in v1:
time: 92.8 us; the launch traced here: 92.6 us
  Pallas kernels  89.5 us (96%)
  local copies, waits for them, and re-layouts  2.68 us (3%)
    pallas_call x1, Pallas kernels, shards(): pl.pallas_call(kernel, out_shape=jax.ShapeDtypeStruct(spectrum.shape, jnp...  89.5 us
    unnamed x9, local copies, waits for them, and re-layouts  2.55 us

profile of v1, /device:TPU:1, one launch (start us, length us, event | category | flops | bytes accessed | tf_op | source)
XLA Modules:
  0.0 92.6 jit_solution(7343685836880761455)
XLA Ops:
  0.1 0.1 fusion.12
  0.2 0.1 multiply_select_fusion.2
  0.3 0.1 multiply_select_fusion
  0.4 0.0 copy-start.1
  0.4 0.0 copy-start.2
  0.4 0.0 copy-start.3
  0.4 0.1 concatenate.3.bins_ref
  0.6 0.6 copy-done.1
  1.2 0.0 copy-done.2
  1.2 0.0 copy-done.3
  1.2 0.0 copy-start
  1.2 1.1 %copy-done = f32[18,64,128]{2,1,0:T(8,128)S(1)} copy-done((f32[18,64,128]{2,1,0:T(8,128)S(1)}, f32[18,64,128]{2,1,0:T(8,128)}, u32[]{:S(2)}) %copy-start) | copy-done | bytes 589848
  2.3 89.5 %shard_map.46 = f32[18,64,128]{2,1,0:T(8,128)S(1)} custom-call(f32[18,64,128]{2,1,0:T(8,128)S(1)} %copy-done, f32[64,128]{1,0:T(8,128)S(1)} %copy-done.1, f32[64,128]{1,0:T(8,128)S(1)} %copy-done.2, s32[64,128]{1,0:T(8,128)S(1)} %copy-done.3, f32[18,10]{1,0:T(8,128)S(1)} %concatenate.3.bins_ref, f32[8,128]{1,0:T(8,128)S(1)} %stack.2.rows_ref), custom_call_target="tpu_custom_call" | custom-call | tf_op jit(solution)/shard_map/pallas_call | solution.py:396
  91.8 0.8 copy.6
  (8 shorter events, 0.1 us)
Async XLA Ops:
  0.4 0.8 copy-start.1
  0.4 0.8 copy-start.2
  0.4 0.8 copy-start.3
  1.2 1.1 %copy-start = (f32[18,64,128]{2,1,0:T(8,128)S(1)}, f32[18,64,128]{2,1,0:T(8,128)}, u32[]{:S(2)}) copy-start(f32[18,64,128]{2,1,0:T(8,128)} %field_hbm.1) | copy-start | bytes 1769476

commit v2 on v1

--- a/solution.py
+++ b/solution.py
@@ -73,15 +73,14 @@
 
 
 def row_table(rows):
-    lines = jnp.arange(rows)
-    coslat = jnp.cos((lines.astype(jnp.float32) - rows / 2 + 0.5) * (0.25 * math.pi / 180.0))
-    masks = [((lines + j >= 0) & (lines + j < rows)).astype(jnp.float32) for j in range(-3, 4)]
-    return jnp.stack([1.0 / coslat] + masks, axis=0)
+    lines = jnp.arange(rows).astype(jnp.float32)
+    coslat = jnp.cos((lines - rows / 2 + 0.5) * (0.25 * math.pi / 180.0))
+    return (1.0 / coslat).reshape(1, rows)
 
 
 def kernel(
     field_hbm, speed_hbm, heading_hbm, flags_hbm, bins_ref, rows_ref, out_ref,
-    first, later, last, got, relay, wide, one, two, speed, heading, flags, gain_x, gain_y, open_sea, ice,
+    first, later, last, got, relay, wide, one, two, lon_taps, lat_taps, speed, heading, flags, gain_x, gain_y, open_sea, ice,
     part, part_in, mid, mid_in, total,
     send_sem, got_sem, leg_send, leg_recv, halo_send, halo_recv,
     a_send, a_recv, b_send, b_recv, c_send, c_recv, in_sem, out_sem,
@@ -89,6 +88,7 @@
     here, columns, rows = field_hbm.shape
     count, sectors = lax.axis_size("bins"), lax.axis_size("lon")
     place, sector = lax.axis_index("bins"), lax.axis_index("lon")
+    ext = columns + 2 * BASE
     line, spot = place // RING, place % RING
     chunk = columns // RING
     def in_row(turn):
@@ -108,6 +108,10 @@
         new = (height + climb + around_z) % around_z
         new_pair = (pair + pair_offset + count // 2) % (count // 2)
         return {"bins": new_pair * 2 + new // (sectors // 2), "lon": new % (sectors // 2) * 2 + core}
+
+    for step in range(STEPS):
+        for rows_of in (pl.ds(0, BASE), pl.ds(BASE + columns, BASE)):
+            wide[step, :, rows_of] = jnp.zeros((here, BASE, rows), jnp.float32)
 
     barrier = pltpu.get_barrier_semaphore()
     partners = [{"bins": across(s * o)} for o in (2, 6, 8) for s in (1, -1)]
@@ -250,28 +254,48 @@
         bottom = 1.0 + bins_ref[b, DAMP] * total[step] + ice[...]
         wide[step, b, pl.ds(BASE, columns)] = jnp.where(flags[...] == 0, 0.0, top / bottom)
 
-    def rate(ref, start, length, lon, lat):
-        centre = ref[pl.ds(start, length)]
-        result = centre * (1.0 + lon[3] + lat[3])
-        for j in (-3, -2, -1, 1, 2, 3):
-            result += ref[pl.ds(start + j, length)] * lon[j + 3]
-            result += pltpu.roll(centre, (-j) % rows, 1) * lat[j + 3]
-        return result
-
-    def advance(step, b, slot):
-        lon = [(PLUS[j] * bins_ref[b, EAST] + MINUS[j] * bins_ref[b, WEST]) * rows_ref[0:1] for j in range(7)]
-        lat = [(PLUS[j] * bins_ref[b, NORTH] + MINUS[j] * bins_ref[b, SOUTH]) * rows_ref[1 + j : 2 + j] for j in range(7)]
-        ext, one_b, two_b = wide.at[step, b], one.at[slot], two.at[slot]
-        around, wider = pl.ds(BASE - 8, columns + 16), columns + 16
-        one_b[around] = rate(ext, BASE - 8, wider, lon, lat)
-        two_b[around] = 0.75 * ext[around] + 0.25 * rate(one_b, BASE - 8, wider, lon, lat)
-        moved = ext[pl.ds(BASE, columns)] / 3.0 + (2.0 / 3.0) * rate(two_b, BASE, columns, lon, lat)
-        moved = jnp.where(flags[...] == 0, 0.0, moved)
-        if step < STEPS - 1:
-            later[b] = moved
-            part[step + 1] += square(b, moved)
-        else:
-            last[b] = moved
+    def halves(values):
+        high = values.astype(jnp.bfloat16)
+        return high, (values - high.astype(jnp.float32)).astype(jnp.bfloat16)
+
+    def rates(fields, bins, signs, rows_out):
+        parts = [halves(field) for field in fields]
+        along_lat = jnp.dot(
+            jnp.concatenate([jnp.concatenate(pair_of, axis=1) for pair_of in parts], axis=0),
+            lat_taps[...], preferred_element_type=jnp.float32,
+        )
+        results = []
+        for i, (field, pair_of, b) in enumerate(zip(fields, parts, bins)):
+            along_lon = jnp.dot(
+                lon_taps[signs[i], rows_out], jnp.concatenate(pair_of, axis=0), preferred_element_type=jnp.float32
+            )
+            start, end = i * ext + rows_out.start, i * ext + rows_out.start + rows_out.size
+            east = (bins_ref[b, EAST] + bins_ref[b, WEST]) * rows_ref[...]
+            results.append(
+                field[rows_out.start : rows_out.start + rows_out.size]
+                + along_lon * east
+                + along_lat[start:end, :rows] * bins_ref[b, NORTH]
+                + along_lat[start:end, rows:] * bins_ref[b, SOUTH]
+            )
+        return results
+
+    def advance(step, group):
+        bins = [group * GROUP + j for j in range(GROUP)]
+        directions = [(place * here + b) // NF for b in bins]
+        signs = [(d + ND // 4) // (ND // 2) % 2 for d in directions]
+        every, inner = pl.ds(0, ext), pl.ds(BASE, columns)
+        for j, values in enumerate(rates([wide[step, b] for b in bins], bins, signs, every)):
+            one[j] = values
+        for j, values in enumerate(rates([one[j] for j in range(GROUP)], bins, signs, every)):
+            two[j] = 0.75 * wide[step, bins[j]] + 0.25 * values
+        for j, values in enumerate(rates([two[j] for j in range(GROUP)], bins, signs, inner)):
+            moved = wide[step, bins[j], inner] * (1.0 / 3.0) + (2.0 / 3.0) * values
+            moved = jnp.where(flags[...] == 0, 0.0, moved)
+            if step < STEPS - 1:
+                later[bins[j]] = moved
+                part[step + 1] += square(bins[j], moved)
+            else:
+                last[bins[j]] = moved
 
     def result_copy(group):
         some = pl.ds(group * GROUP, GROUP)
@@ -293,6 +317,19 @@
     inputs = [pltpu.make_async_copy(src, dst, in_sem.at[i]) for i, (src, dst) in enumerate(inputs)]
     for copy in inputs:
         copy.start()
+
+    def band(shape, along, across_it, taps):
+        offset = lax.broadcasted_iota(jnp.int32, shape, along) - lax.broadcasted_iota(jnp.int32, shape, across_it)
+        matrix = jnp.zeros(shape, jnp.float32)
+        for j, tap in enumerate(taps):
+            matrix = jnp.where(offset == j - 3, tap, matrix)
+        return matrix.astype(jnp.bfloat16)
+
+    for sign, taps in enumerate((PLUS, MINUS)):
+        lon_band, lat_band = band((ext, ext), 1, 0, taps), band((rows, rows), 0, 1, taps)
+        lon_taps[sign] = jnp.concatenate([lon_band, lon_band], axis=1)
+        for half in range(2):
+            lat_taps[pl.ds(half * rows, rows), pl.ds(sign * rows, rows)] = lat_band
     for step in range(1, STEPS):
         part[step] = jnp.zeros((columns, rows), jnp.float32)
     inputs[0].wait()
@@ -354,8 +391,7 @@
                 group = (g - LAG + FIRST_GROUP[step]) % GROUPS
                 for side in range(2):
                     halo_copy(step, group, side).wait_recv()
-                for j in range(GROUP):
-                    advance(step, group * GROUP + j, j)
+                advance(step, group)
                 if step < STEPS - 1:
                     send_group(step + 1, group)
                 else:
@@ -407,6 +443,8 @@
             buffer(STEPS, here, ext, rows),
             buffer(GROUP, ext, rows),
             buffer(GROUP, ext, rows),
+            pltpu.VMEM((2, ext, 2 * ext), jnp.bfloat16),
+            pltpu.VMEM((2 * rows, 2 * rows), jnp.bfloat16),
             buffer(*whole),
             buffer(*whole),
             pltpu.VMEM(whole, jnp.int32),
@@ -426,7 +464,7 @@
         + [dma((STEPS, RING))] * 6
         + [dma((4,)), dma((GROUPS,))],
         compiler_params=pltpu.CompilerParams(
-            collective_id=0, has_side_effects=True, vmem_limit_bytes=24 * 1024 * 1024
+            collective_id=0, has_side_effects=True, vmem_limit_bytes=56 * 1024 * 1024
         ),
     )(spectrum, wind_speed, wind_dir, flags, bin_table(index), row_table(rows))
 

time: 92.8 us -> 90.9 us (0.980)
  Pallas kernels: 89.5 us -> 86.8 us
    pallas_call x1, Pallas kernels: 89.5 us -> 86.8 us  [shards(): pl.pallas_call(kernel, out_shape=jax.ShapeDtypeStruct(spectrum.shape, jnp...]
    unnamed x9 -> x1, local copies, waits for them, and re-layouts: 2.55 us -> 1.93 us
where the time goes in v2:
time: 90.9 us; the launch traced here: 90.3 us
  Pallas kernels  86.8 us (95%)
  local copies, waits for them, and re-layouts  2.63 us (3%)
    pallas_call x1, Pallas kernels, shards(): pl.pallas_call(kernel, out_shape=jax.ShapeDtypeStruct(spectrum.shape, jnp...  86.8 us
    unnamed x1, local copies, waits for them, and re-layouts  1.93 us

profile of v2, /device:TPU:1, one launch (start us, length us, event | category | flops | bytes accessed | tf_op | source)
XLA Modules:
  0.0 90.3 jit_solution(2615125352166991972)
XLA Ops:
  0.0 0.6 cosine_divide_fusion.rows_ref
  0.6 0.1 fusion.12
  0.7 0.1 multiply_select_fusion.2
  0.8 0.1 multiply_select_fusion
  0.9 0.7 concatenate.3.bins_ref
  1.6 86.8 %shard_map.46 = f32[18,64,128]{2,1,0:T(8,128)} custom-call(f32[18,64,128]{2,1,0:T(8,128)} %field_hbm.1, f32[64,128]{1,0:T(8,128)} %speed_hbm.1, f32[64,128]{1,0:T(8,128)} %heading_hbm.1, s32[64,128]{1,0:T(8,128)} %flags_hbm.1, f32[18,10]{1,0:T(8,128)} %concatenate.3.bins_ref, f32[1,128]{1,0:T(1,128)} %cosine_divide_fusion.rows_ref), custom_call_target="tpu_custom_call" | custom-call | tf_op jit(solution)/shard_map/pallas_call | solution.py:432
  88.4 1.9 %copy.6 = f32[18,64,128]{2,1,0:T(8,128)} copy(f32[18,64,128]{2,1,0:T(8,128)} %shard_map.46) | data formatting | bytes 1179648
  (2 shorter events, 0.0 us)

commit v3 on v1

--- a/solution.py
+++ b/solution.py
@@ -73,15 +73,91 @@
 
 
 def row_table(rows):
-    lines = jnp.arange(rows)
-    coslat = jnp.cos((lines.astype(jnp.float32) - rows / 2 + 0.5) * (0.25 * math.pi / 180.0))
-    masks = [((lines + j >= 0) & (lines + j < rows)).astype(jnp.float32) for j in range(-3, 4)]
-    return jnp.stack([1.0 / coslat] + masks, axis=0)
+    lines = jnp.arange(rows).astype(jnp.float32)
+    coslat = jnp.cos((lines - rows / 2 + 0.5) * (0.25 * math.pi / 180.0))
+    return (1.0 / coslat).reshape(1, rows)
+
+
+def halves(values):
+    high = values.astype(jnp.bfloat16)
+    return high, (values - high.astype(jnp.float32)).astype(jnp.bfloat16)
+
+def rates(fields, bins, signs, rows_out, lon_taps, lat_taps, bins_ref, rows_ref):
+    ext, rows = fields[0].shape
+    parts = [halves(field) for field in fields]
+    along_lat = jnp.dot(
+        jnp.concatenate([jnp.concatenate(pair_of, axis=1) for pair_of in parts], axis=0),
+        lat_taps[...], preferred_element_type=jnp.float32,
+    )
+    results = []
+    for i, (field, pair_of, b) in enumerate(zip(fields, parts, bins)):
+        along_lon = jnp.dot(
+            lon_taps[signs[i], rows_out], jnp.concatenate(pair_of, axis=0), preferred_element_type=jnp.float32
+        )
+        start, end = i * ext + rows_out.start, i * ext + rows_out.start + rows_out.size
+        east = (bins_ref[b, EAST] + bins_ref[b, WEST]) * rows_ref[...]
+        results.append(
+            field[rows_out.start : rows_out.start + rows_out.size]
+            + along_lon * east
+            + along_lat[start:end, :rows] * bins_ref[b, NORTH]
+            + along_lat[start:end, rows:] * bins_ref[b, SOUTH]
+        )
+    return results
+
+
+def sections(place, here, start, bins, lon_taps, lat_taps, bins_ref, rows_ref, one, two):
+    ext, rows = one.shape[1:]
+    count = len(bins)
+    directions = [(place * here + b) // NF for b in bins]
+    signs = [(d + ND // 4) // (ND // 2) % 2 for d in directions]
+    every, inner = pl.ds(0, ext), pl.ds(BASE, ext - 2 * BASE)
+    tables = lon_taps, lat_taps, bins_ref, rows_ref
+    for j, values in enumerate(rates([start(j) for j in range(count)], bins, signs, every, *tables)):
+        one[j] = values
+    for j, values in enumerate(rates([one[j] for j in range(count)], bins, signs, every, *tables)):
+        two[j] = 0.75 * start(j) + 0.25 * values
+    results = rates([two[j] for j in range(count)], bins, signs, inner, *tables)
+    return [
+        start(j)[BASE : ext - BASE] * (1.0 / 3.0) + (2.0 / 3.0) * values for j, values in enumerate(results)
+    ]
+
+
+def fill_taps(lon_taps, lat_taps):
+    ext, rows = lon_taps.shape[1], lat_taps.shape[0] // 2
+
+    def band(shape, along, across_it, taps):
+        offset = lax.broadcasted_iota(jnp.int32, shape, along) - lax.broadcasted_iota(jnp.int32, shape, across_it)
+        matrix = jnp.zeros(shape, jnp.float32)
+        for j, tap in enumerate(taps):
+            matrix = jnp.where(offset == j - 3, tap, matrix)
+        return matrix.astype(jnp.bfloat16)
+
+    for sign, taps in enumerate((PLUS, MINUS)):
+        lon_band, lat_band = band((ext, ext), 1, 0, taps), band((rows, rows), 0, 1, taps)
+        lon_taps[sign] = jnp.concatenate([lon_band, lon_band], axis=1)
+        for half in range(2):
+            lat_taps[pl.ds(half * rows, rows), pl.ds(sign * rows, rows)] = lat_band
+
+
+def last_kernel(wide, flags, bins_ref, rows_ref, out_ref, one, two, lon_taps, lat_taps):
+    step = pl.program_id(0)
+    place = lax.axis_index("bins")
+
+    @pl.when(step == 0)
+    def _():
+        fill_taps(lon_taps, lat_taps)
+
+    bins = [step * GROUP + j for j in range(GROUP)]
+    results = sections(
+        place, GROUP * GROUPS, lambda j: wide[j], bins, lon_taps, lat_taps, bins_ref, rows_ref, one, two
+    )
+    for j, moved in enumerate(results):
+        out_ref[j] = jnp.where(flags[...] == 0, 0.0, moved)
 
 
 def kernel(
     field_hbm, speed_hbm, heading_hbm, flags_hbm, bins_ref, rows_ref, out_ref,
-    first, later, last, got, relay, wide, one, two, speed, heading, flags, gain_x, gain_y, open_sea, ice,
+    first, later, got, relay, wide, one, two, lon_taps, lat_taps, speed, heading, flags, gain_x, gain_y, open_sea, ice,
     part, part_in, mid, mid_in, total,
     send_sem, got_sem, leg_send, leg_recv, halo_send, halo_recv,
     a_send, a_recv, b_send, b_recv, c_send, c_recv, in_sem, out_sem,
@@ -89,6 +165,7 @@
     here, columns, rows = field_hbm.shape
     count, sectors = lax.axis_size("bins"), lax.axis_size("lon")
     place, sector = lax.axis_index("bins"), lax.axis_index("lon")
+    ext = columns + 2 * BASE
     line, spot = place // RING, place % RING
     chunk = columns // RING
     def in_row(turn):
@@ -108,6 +185,10 @@
         new = (height + climb + around_z) % around_z
         new_pair = (pair + pair_offset + count // 2) % (count // 2)
         return {"bins": new_pair * 2 + new // (sectors // 2), "lon": new % (sectors // 2) * 2 + core}
+
+    for step in range(STEPS):
+        for rows_of in (pl.ds(0, BASE), pl.ds(BASE + columns, BASE)):
+            wide[step, :, rows_of] = jnp.zeros((here, BASE, rows), jnp.float32)
 
     barrier = pltpu.get_barrier_semaphore()
     partners = [{"bins": across(s * o)} for o in (2, 6, 8) for s in (1, -1)]
@@ -250,32 +331,19 @@
         bottom = 1.0 + bins_ref[b, DAMP] * total[step] + ice[...]
         wide[step, b, pl.ds(BASE, columns)] = jnp.where(flags[...] == 0, 0.0, top / bottom)
 
-    def rate(ref, start, length, lon, lat):
-        centre = ref[pl.ds(start, length)]
-        result = centre * (1.0 + lon[3] + lat[3])
-        for j in (-3, -2, -1, 1, 2, 3):
-            result += ref[pl.ds(start + j, length)] * lon[j + 3]
-            result += pltpu.roll(centre, (-j) % rows, 1) * lat[j + 3]
-        return result
-
-    def advance(step, b, slot):
-        lon = [(PLUS[j] * bins_ref[b, EAST] + MINUS[j] * bins_ref[b, WEST]) * rows_ref[0:1] for j in range(7)]
-        lat = [(PLUS[j] * bins_ref[b, NORTH] + MINUS[j] * bins_ref[b, SOUTH]) * rows_ref[1 + j : 2 + j] for j in range(7)]
-        ext, one_b, two_b = wide.at[step, b], one.at[slot], two.at[slot]
-        around, wider = pl.ds(BASE - 8, columns + 16), columns + 16
-        one_b[around] = rate(ext, BASE - 8, wider, lon, lat)
-        two_b[around] = 0.75 * ext[around] + 0.25 * rate(one_b, BASE - 8, wider, lon, lat)
-        moved = ext[pl.ds(BASE, columns)] / 3.0 + (2.0 / 3.0) * rate(two_b, BASE, columns, lon, lat)
-        moved = jnp.where(flags[...] == 0, 0.0, moved)
-        if step < STEPS - 1:
-            later[b] = moved
-            part[step + 1] += square(b, moved)
-        else:
-            last[b] = moved
+    def advance(step, group):
+        bins = [group * GROUP + j for j in range(GROUP)]
+        results = sections(
+            place, here, lambda j: wide[step, bins[j]], bins, lon_taps, lat_taps, bins_ref, rows_ref, one, two
+        )
+        for j, moved in enumerate(results):
+            moved = jnp.where(flags[...] == 0, 0.0, moved)
+            later[bins[j]] = moved
+            part[step + 1] += square(bins[j], moved)
 
     def result_copy(group):
         some = pl.ds(group * GROUP, GROUP)
-        return pltpu.make_async_copy(last.at[some], out_ref.at[some], out_sem.at[group])
+        return pltpu.make_async_copy(wide.at[STEPS - 1, some], out_ref.at[some], out_sem.at[group])
 
     def send_group(step, group):
         for k in range(GROUPS):
@@ -293,6 +361,8 @@
     inputs = [pltpu.make_async_copy(src, dst, in_sem.at[i]) for i, (src, dst) in enumerate(inputs)]
     for copy in inputs:
         copy.start()
+
+    fill_taps(lon_taps, lat_taps)
     for step in range(1, STEPS):
         part[step] = jnp.zeros((columns, rows), jnp.float32)
     inputs[0].wait()
@@ -354,9 +424,8 @@
                 group = (g - LAG + FIRST_GROUP[step]) % GROUPS
                 for side in range(2):
                     halo_copy(step, group, side).wait_recv()
-                for j in range(GROUP):
-                    advance(step, group * GROUP + j, j)
                 if step < STEPS - 1:
+                    advance(step, group)
                     send_group(step + 1, group)
                 else:
                     result_copy(group).start()
@@ -393,13 +462,13 @@
     def buffer(*shape):
         return pltpu.VMEM(shape, jnp.float32)
 
-    return pl.pallas_call(
+    bins_of, rows_of = bin_table(index), row_table(rows)
+    sourced = pl.pallas_call(
         kernel,
-        out_shape=jax.ShapeDtypeStruct(spectrum.shape, jnp.float32),
+        out_shape=jax.ShapeDtypeStruct((here, ext, rows), jnp.float32),
         in_specs=[hbm] * 4 + [pl.BlockSpec(memory_space=pltpu.SMEM), pl.BlockSpec(memory_space=pltpu.VMEM)],
         out_specs=hbm,
         scratch_shapes=[
-            buffer(here, *whole),
             buffer(here, *whole),
             buffer(here, *whole),
             buffer(STEPS, 2, here, *whole),
@@ -407,6 +476,8 @@
             buffer(STEPS, here, ext, rows),
             buffer(GROUP, ext, rows),
             buffer(GROUP, ext, rows),
+            pltpu.VMEM((2, ext, 2 * ext), jnp.bfloat16),
+            pltpu.VMEM((2 * rows, 2 * rows), jnp.bfloat16),
             buffer(*whole),
             buffer(*whole),
             pltpu.VMEM(whole, jnp.int32),
@@ -426,9 +497,28 @@
         + [dma((STEPS, RING))] * 6
         + [dma((4,)), dma((GROUPS,))],
         compiler_params=pltpu.CompilerParams(
-            collective_id=0, has_side_effects=True, vmem_limit_bytes=24 * 1024 * 1024
+            collective_id=0, has_side_effects=True, vmem_limit_bytes=56 * 1024 * 1024
         ),
-    )(spectrum, wind_speed, wind_dir, flags, bin_table(index), row_table(rows))
+    )(spectrum, wind_speed, wind_dir, flags, bins_of, rows_of)
+    return pl.pallas_call(
+        last_kernel,
+        grid=(GROUPS,),
+        out_shape=jax.ShapeDtypeStruct(spectrum.shape, jnp.float32),
+        in_specs=[
+            pl.BlockSpec((GROUP, ext, rows), lambda i: (i, 0, 0)),
+            pl.BlockSpec(whole, lambda i: (0, 0)),
+            pl.BlockSpec(memory_space=pltpu.SMEM),
+            pl.BlockSpec((1, rows), lambda i: (0, 0)),
+        ],
+        out_specs=pl.BlockSpec((GROUP, *whole), lambda i: (i, 0, 0)),
+        scratch_shapes=[
+            buffer(GROUP, ext, rows),
+            buffer(GROUP, ext, rows),
+            pltpu.VMEM((2, ext, 2 * ext), jnp.bfloat16),
+            pltpu.VMEM((2 * rows, 2 * rows), jnp.bfloat16),
+        ],
+        compiler_params=pltpu.CompilerParams(vmem_limit_bytes=56 * 1024 * 1024),
+    )(sourced, flags, bins_of, rows_of)
 
 
 def solution(mesh):

time: 92.8 us -> 93.3 us (level); the launches traced: 92.6 us -> 91.5 us
  local copies, waits for them, and re-layouts: 2.68 us -> 0.7 us
    unnamed x9 -> x0, local copies, waits for them, and re-layouts: 2.55 us -> none
    pallas_call x1 -> x2, Pallas kernels: 89.5 us -> 89.9 us  [the longest x1 83.6 us: shards(): pl.pallas_call(kernel, out_shape=jax.ShapeDtypeStruct((here, ext, rows),...]
where the time goes in v3:
time: 93.3 us; the launch traced here: 91.5 us
  Pallas kernels  89.9 us (96%)
    pallas_call x1, Pallas kernels, shards(): pl.pallas_call(kernel, out_shape=jax.ShapeDtypeStruct((here, ext, rows),...  83.6 us
    pallas_call x1, Pallas kernels, shards(): pl.pallas_call(last_kernel, grid=(GROUPS,), out_shape=jax.ShapeDtypeStruc...  6.22 us

profile of v3, /device:TPU:1, one launch (start us, length us, event | category | flops | bytes accessed | tf_op | source)
XLA Modules:
  0.0 91.5 jit_solution(8894940548387684511)
XLA Ops:
  0.0 0.6 cosine_divide_fusion.rows_ref
  0.6 0.1 fusion.12
  0.7 0.1 multiply_select_fusion.2
  0.8 0.1 multiply_select_fusion
  0.9 0.7 concatenate.3.bins_ref
  1.6 83.6 %shard_map.46.wide = f32[18,96,128]{2,1,0:T(8,128)} custom-call(f32[18,64,128]{2,1,0:T(8,128)} %field_hbm.1, f32[64,128]{1,0:T(8,128)} %speed_hbm.1, f32[64,128]{1,0:T(8,128)} %heading_hbm.1, s32[64,128]{1,0:T(8,128)} %flags.1, f32[18,10]{1,0:T(8,128)} %concatenate.3.bins_ref, f32[1,128]{1,0:T(1,128)} %cosine_divide_fusion.rows_ref), custom_call_target="tpu_custom_call" | custom-call | tf_op jit(solution)/shard_map/pallas_call | solution.py:466
  85.3 6.2 %shard_map.47 = f32[18,64,128]{2,1,0:T(8,128)} custom-call(f32[18,96,128]{2,1,0:T(8,128)} %shard_map.46.wide, s32[64,128]{1,0:T(8,128)} %flags.1, f32[18,10]{1,0:T(8,128)} %concatenate.3.bins_ref, f32[1,128]{1,0:T(1,128)} %cosine_divide_fusion.rows_ref), custom_call_target="tpu_custom_call" | custom-call | tf_op jit(solution)/shard_map/pallas_call | solution.py:503
  (2 shorter events, 0.0 us)

commit v4 on v2

--- a/solution.py
+++ b/solution.py
@@ -34,7 +34,6 @@
 )
 SHARED = ((3, 12, 2, 0), (4, 14, 3, 2), (5, 17, 1, 5))
 FAR = ((0, 16, 2, 0, -1), (1, 0, 3, 8, 1), (1, 3, 3, 11, -1), (1, 6, 3, 14, 1), (1, 9, 1, 17, -1))
-KEPT_BACK = (1, 2)
 S0, F0 = len(DIRECT), len(DIRECT) + len(SHARED)
 PIECES = F0 + len(FAR)
 NEEDS = (
@@ -176,9 +175,9 @@
             leg(step, piece).wait_recv()
             second_leg(step, piece).start()
 
-    def pass_on_shared(step):
-        for piece, (before, *_) in enumerate(SHARED):
-            direct(step, before).wait_recv()
+    def pass_on_shared(step, pieces):
+        for piece in pieces:
+            direct(step, SHARED[piece][0]).wait_recv()
             shared(step, piece).start()
 
     def halo_copy(step, group, side):
@@ -193,22 +192,22 @@
             {"lon": (sector + turn + sectors) % sectors},
         )
 
+    def chunk_of(owner):
+        return pl.ds(pl.multiple_of(owner * chunk, chunk), chunk)
+
     def a_copy(step, turn):
-        start = pl.multiple_of((spot + turn) % RING * chunk, chunk)
-        return send(part.at[step, pl.ds(start, chunk)], part_in.at[step, turn], a_send.at[step, turn], a_recv.at[step, turn], {"bins": in_row(turn)})
+        return send(part.at[step, chunk_of((line + turn) % RING)], part_in.at[step, turn], a_send.at[step, turn], a_recv.at[step, turn], {"bins": in_column(turn)})
 
     def b_copy(step, turn):
-        return send(mid.at[step], mid_in.at[step, turn], b_send.at[step, turn], b_recv.at[step, turn], {"bins": in_column(turn)})
+        return send(mid.at[step], mid_in.at[step, turn], b_send.at[step, turn], b_recv.at[step, turn], {"bins": in_row(turn)})
 
     def c_copy(step, turn):
-        start = pl.multiple_of(spot * chunk, chunk)
-        mine = total.at[step, pl.ds(start, chunk)]
-        return send(mine, mine, c_send.at[step, turn], c_recv.at[step, turn], {"bins": in_row(turn)})
+        mine = total.at[step, chunk_of(line)]
+        return send(mine, mine, c_send.at[step, turn], c_recv.at[step, turn], {"bins": in_column(turn)})
 
     def c_from(step, turn):
-        start = pl.multiple_of((spot + RING - turn) % RING * chunk, chunk)
-        theirs = total.at[step, pl.ds(start, chunk)]
-        return send(theirs, theirs, c_send.at[step, turn], c_recv.at[step, turn], {"bins": in_row(turn)})
+        theirs = total.at[step, chunk_of((line + RING - turn) % RING)]
+        return send(theirs, theirs, c_send.at[step, turn], c_recv.at[step, turn], {"bins": in_column(turn)})
 
     def square(b, values):
         scaled = bins_ref[b, RATIO] * values
@@ -219,8 +218,7 @@
             a_copy(step, turn).start()
 
     def spread_b(step):
-        start = pl.multiple_of(spot * chunk, chunk)
-        so_far = part[step, pl.ds(start, chunk)]
+        so_far = part[step, chunk_of(line)]
         for turn in range(1, RING):
             a_copy(step, turn).wait_recv()
             so_far += part_in[step, turn]
@@ -229,12 +227,11 @@
             b_copy(step, turn).start()
 
     def spread_c(step):
-        start = pl.multiple_of(spot * chunk, chunk)
         so_far = mid[step]
         for turn in range(1, RING):
             b_copy(step, turn).wait_recv()
             so_far += mid_in[step, turn]
-        total[step, pl.ds(start, chunk)] = so_far
+        total[step, chunk_of(line)] = so_far
         for turn in range(1, RING):
             c_copy(step, turn).start()
 
@@ -310,7 +307,7 @@
                     if b in mine:
                         leg(step, piece).start()
                 for piece, (_, b, *_) in enumerate(DIRECT):
-                    if b in mine and piece not in KEPT_BACK:
+                    if b in mine:
                         direct(step, piece).start()
 
     inputs = [(field_hbm, first), (speed_hbm, speed), (heading_hbm, heading), (flags_hbm, flags)]
@@ -339,7 +336,7 @@
     spread_a(0)
     for piece in range(len(FAR)):
         leg(0, piece).start()
-    for piece in (3, 4, 5, 6, 0):
+    for piece in (3, 4, 5, 6, 0, 1, 2):
         direct(0, piece).start()
     for copy in inputs[1:]:
         copy.wait()
@@ -349,25 +346,21 @@
     open_sea[...] = jnp.where(flags[...] == 1, 1.0, 0.0)
     ice[...] = jnp.where(flags[...] == 2, ice_loss, 0.0)
     spread_b(0)
-    direct(0, 1).start()
     pass_on_far(0, (0, 1, 2))
+    pass_on_shared(0, range(len(SHARED)))
+    pass_on_far(0, (3, 4))
     spread_c(0)
-    direct(0, 2).start()
-    pass_on_far(0, (3, 4))
-    pass_on_shared(0)
     spread_end(0)
 
     for step in range(STEPS):
         if step > 0:
             spread_a(step)
-            direct(step, 1).start()
-            pass_on_far(step, (1, 2))
+            pass_on_far(step, (4,))
+            pass_on_shared(step, (0,))
             spread_b(step)
-            direct(step, 2).start()
-            pass_on_far(step, (3, 4))
-            pass_on_shared(step)
+            pass_on_shared(step, (1, 2))
+            pass_on_far(step, (0,))
             spread_c(step)
-            pass_on_far(step, (0,))
             spread_end(step)
 
         @pl.loop(0, GROUPS + LAG)
@@ -385,6 +378,12 @@
                     source(step, group * GROUP + j)
                 for side in range(2):
                     halo_copy(step, group, side).start()
+
+            if step < STEPS - 1:
+                for piece in (1, 2, 3):
+                    @pl.when(g == piece + 4)
+                    def _(piece=piece):
+                        pass_on_far(step + 1, (piece,))
 
             @pl.when(g >= LAG)
             def _():

time: 90.9 us -> 102 us (1.12)
  the two profiles are of different devices: /device:TPU:1 before, /device:TPU:8 now
where the time goes in v4:
time: 102 us
  Pallas kernels  98.1 us (96%)
  local copies, waits for them, and re-layouts  2.63 us (3%)
    pallas_call x1, Pallas kernels, shards(): pl.pallas_call(kernel, out_shape=jax.ShapeDtypeStruct(spectrum.shape, jnp...  98.1 us

profile of v4, /device:TPU:8, one launch (start us, length us, event | category | flops | bytes accessed | tf_op | source)
XLA Modules:
  0.0 101.7 jit_solution(16279120470234611735)
XLA Ops:
  0.0 0.6 cosine_divide_fusion.rows_ref
  0.6 0.1 fusion.12
  0.7 0.1 multiply_select_fusion.2
  0.8 0.1 multiply_select_fusion
  0.9 0.7 concatenate.3.bins_ref
  1.6 98.1 %shard_map.46 = f32[18,64,128]{2,1,0:T(8,128)} custom-call(f32[18,64,128]{2,1,0:T(8,128)} %field_hbm.1, f32[64,128]{1,0:T(8,128)} %speed_hbm.1, f32[64,128]{1,0:T(8,128)} %heading_hbm.1, s32[64,128]{1,0:T(8,128)} %flags_hbm.1, f32[18,10]{1,0:T(8,128)} %concatenate.3.bins_ref, f32[1,128]{1,0:T(1,128)} %cosine_divide_fusion.rows_ref), custom_call_target="tpu_custom_call" | custom-call | tf_op jit(solution)/shard_map/pallas_call | solution.py:431
  99.7 1.9 %copy.6 = f32[18,64,128]{2,1,0:T(8,128)} copy(f32[18,64,128]{2,1,0:T(8,128)} %shard_map.46) | data formatting | bytes 1179648
  (2 shorter events, 0.0 us)

commit v5 on v2

--- a/solution.py
+++ b/solution.py
@@ -1,8 +1,8 @@
-import functools
 import math
 
 import jax
 import jax.numpy as jnp
+import numpy as np
 from jax import lax
 from jax.experimental import pallas as pl
 from jax.experimental.pallas import tpu as pltpu
@@ -18,7 +18,7 @@
 ice_loss = 1.0
 courant = 0.6
 
-RING = 8
+LINES, ROW = 8, 4
 HALO = 9
 BASE = 16
 GROUP = 3
@@ -46,56 +46,60 @@
 RATIO, COS, SIN, DAMP, UPPER, LOWER, EAST, WEST, NORTH, SOUTH = range(10)
 
 
-def bin_table(index):
-    direction = (index // NF).astype(jnp.float32)
-    level = (index % NF).astype(jnp.float32)
-    theta = direction * (2.0 * math.pi / ND)
-    ratio = jnp.power(1.05, level - NF // 2)
-    group = jnp.power(1.1, -level)
-    east = courant * group * jnp.cos(theta)
-    north = courant * group * jnp.sin(theta)
-    ratio, theta, east, north, level = (v[:, None] for v in (ratio, theta, east, north, level))
-    return jnp.concatenate(
-        [
-            ratio,
-            jnp.cos(theta),
-            jnp.sin(theta),
-            break_gain * ratio * ratio / (NF * ND),
-            (level + 2 < NF).astype(jnp.float32),
-            (level >= 2).astype(jnp.float32),
-            jnp.where(east >= 0.0, east / -60.0, 0.0),
-            jnp.where(east >= 0.0, 0.0, east / -60.0),
-            jnp.where(north >= 0.0, north / -60.0, 0.0),
-            jnp.where(north >= 0.0, 0.0, north / -60.0),
-        ],
-        axis=1,
+def bin_table(places, here):
+    index = np.arange(places * here).reshape(places, here)
+    theta = (index // NF).astype(np.float32) * np.float32(2.0 * math.pi / ND)
+    theta = theta.astype(np.float64)
+    level = index % NF
+    ratio = 1.05 ** (level - NF // 2.0)
+    east = courant * 1.1 ** (-level.astype(np.float64)) * np.cos(theta)
+    north = courant * 1.1 ** (-level.astype(np.float64)) * np.sin(theta)
+    table = np.zeros((places, 16, 128), np.float32)
+    values = (
+        ratio,
+        np.cos(theta),
+        np.sin(theta),
+        break_gain * ratio * ratio / (NF * ND),
+        level + 2 < NF,
+        level >= 2,
+        np.maximum(east, 0.0) / -60.0,
+        np.minimum(east, 0.0) / -60.0,
+        np.maximum(north, 0.0) / -60.0,
+        np.minimum(north, 0.0) / -60.0,
     )
+    for quantity, value in enumerate(values):
+        table[:, quantity, :here] = value
+    return table
 
 
 def row_table(rows):
-    lines = jnp.arange(rows).astype(jnp.float32)
-    coslat = jnp.cos((lines - rows / 2 + 0.5) * (0.25 * math.pi / 180.0))
-    return (1.0 / coslat).reshape(1, rows)
+    lines = np.arange(rows)
+    coslat = np.cos((lines - rows / 2 + 0.5) * (0.25 * math.pi / 180.0))
+    return np.broadcast_to(1.0 / coslat, (8, rows)).astype(np.float32)
 
 
 def kernel(
-    field_hbm, speed_hbm, heading_hbm, flags_hbm, bins_ref, rows_ref, out_ref,
-    first, later, last, got, relay, wide, one, two, lon_taps, lat_taps, speed, heading, flags, gain_x, gain_y, open_sea, ice,
-    part, part_in, mid, mid_in, total,
+    field_hbm, speed_hbm, heading_hbm, flags_hbm, bins_hbm, rows_hbm, out_ref,
+    first, later, last, got, relay, wide, one, two, lon_taps, lat_taps, bins_ref, rows_ref, speed, heading, flags, gain_x, gain_y, open_sea, ice,
+    part, part_in, half, half_in, mid, mid_in, total,
     send_sem, got_sem, leg_send, leg_recv, halo_send, halo_recv,
-    a_send, a_recv, b_send, b_recv, c_send, c_recv, in_sem, out_sem,
+    a_send, a_recv, z_send, z_recv, b_send, b_recv, c_send, c_recv, in_sem, out_sem,
 ):
     here, columns, rows = field_hbm.shape
     count, sectors = lax.axis_size("bins"), lax.axis_size("lon")
     place, sector = lax.axis_index("bins"), lax.axis_index("lon")
     ext = columns + 2 * BASE
-    line, spot = place // RING, place % RING
-    chunk = columns // RING
+    line, spot = place // (2 * ROW), place // 2 % ROW
+    chunk = columns // ROW
+
     def in_row(turn):
-        return line * RING + (spot + turn) % RING
+        return (line * ROW + (spot + turn) % ROW) * 2 + place % 2
 
     def in_column(turn):
-        return (line + turn) % RING * RING + spot
+        return ((line + turn) % LINES * ROW + spot) * 2 + place % 2
+
+    def opposite():
+        return place + 1 - 2 * (place % 2)
 
     def across(offset):
         return (place + offset + count) % count
@@ -114,10 +118,11 @@
             wide[step, :, rows_of] = jnp.zeros((here, BASE, rows), jnp.float32)
 
     barrier = pltpu.get_barrier_semaphore()
-    partners = [{"bins": across(s * o)} for o in (2, 6, 8) for s in (1, -1)]
+    partners = [{"bins": across(s * o)} for o in (2, 6) for s in (1, -1)]
     partners += [at(o, s * LEG) for o in (-3, -1, 0, 1, 3) for s in (1, -1)]
-    partners += [{"bins": in_row(t)} for t in range(1, RING)]
-    partners += [{"bins": in_column(t)} for t in range(1, RING)]
+    partners += [{"bins": in_row(t)} for t in range(1, ROW)]
+    partners += [{"bins": in_column(t)} for t in range(1, LINES)]
+    partners += [{"bins": opposite()}]
     partners += [{"lon": (sector + s + sectors) % sectors} for s in (1, -1)]
     for partner in partners:
         pl.semaphore_signal(barrier, inc=1, device_id=partner, device_id_type=pl.DeviceIdType.MESH)
@@ -193,65 +198,71 @@
             {"lon": (sector + turn + sectors) % sectors},
         )
 
+    def chunk_of(owner):
+        return pl.ds(pl.multiple_of(owner * chunk, chunk), chunk)
+
     def a_copy(step, turn):
-        start = pl.multiple_of((spot + turn) % RING * chunk, chunk)
-        return send(part.at[step, pl.ds(start, chunk)], part_in.at[step, turn], a_send.at[step, turn], a_recv.at[step, turn], {"bins": in_row(turn)})
+        return send(part.at[step, chunk_of((spot + turn) % ROW)], part_in.at[step, turn], a_send.at[step, turn], a_recv.at[step, turn], {"bins": in_row(turn)})
+
+    def z_copy(step):
+        return send(half.at[step], half_in.at[step], z_send.at[step], z_recv.at[step], {"bins": opposite()})
 
     def b_copy(step, turn):
         return send(mid.at[step], mid_in.at[step, turn], b_send.at[step, turn], b_recv.at[step, turn], {"bins": in_column(turn)})
 
     def c_copy(step, turn):
-        start = pl.multiple_of(spot * chunk, chunk)
-        mine = total.at[step, pl.ds(start, chunk)]
+        mine = total.at[step, chunk_of(spot)]
         return send(mine, mine, c_send.at[step, turn], c_recv.at[step, turn], {"bins": in_row(turn)})
 
     def c_from(step, turn):
-        start = pl.multiple_of((spot + RING - turn) % RING * chunk, chunk)
-        theirs = total.at[step, pl.ds(start, chunk)]
+        theirs = total.at[step, chunk_of((spot + ROW - turn) % ROW)]
         return send(theirs, theirs, c_send.at[step, turn], c_recv.at[step, turn], {"bins": in_row(turn)})
 
     def square(b, values):
-        scaled = bins_ref[b, RATIO] * values
+        scaled = bins_ref[RATIO, b] * values
         return scaled * scaled
 
     def spread_a(step):
-        for turn in range(1, RING):
+        for turn in range(1, ROW):
             a_copy(step, turn).start()
 
-    def spread_b(step):
-        start = pl.multiple_of(spot * chunk, chunk)
-        so_far = part[step, pl.ds(start, chunk)]
-        for turn in range(1, RING):
+    def spread_z(step):
+        so_far = part[step, chunk_of(spot)]
+        for turn in range(1, ROW):
             a_copy(step, turn).wait_recv()
             so_far += part_in[step, turn]
-        mid[step] = so_far
-        for turn in range(1, RING):
+        half[step] = so_far
+        z_copy(step).start()
+
+    def spread_b(step):
+        z_copy(step).wait_recv()
+        mid[step] = half[step] + half_in[step]
+        for turn in range(1, LINES):
             b_copy(step, turn).start()
 
     def spread_c(step):
-        start = pl.multiple_of(spot * chunk, chunk)
         so_far = mid[step]
-        for turn in range(1, RING):
+        for turn in range(1, LINES):
             b_copy(step, turn).wait_recv()
             so_far += mid_in[step, turn]
-        total[step, pl.ds(start, chunk)] = so_far
-        for turn in range(1, RING):
+        total[step, chunk_of(spot)] = so_far
+        for turn in range(1, ROW):
             c_copy(step, turn).start()
 
     def spread_end(step):
-        for turn in range(1, RING):
+        for turn in range(1, ROW):
             c_from(step, turn).wait_recv()
 
     def source(step, b):
         energy = field_of(step)[b]
-        above = got[step, 0, b] * bins_ref[b, UPPER]
-        below = got[step, 1, b] * bins_ref[b, LOWER]
-        ratio = bins_ref[b, RATIO]
-        wind = jnp.maximum(bins_ref[b, COS] * gain_x[...] + bins_ref[b, SIN] * gain_y[...], 0.0)
+        above = got[step, 0, b] * bins_ref[UPPER, b]
+        below = got[step, 1, b] * bins_ref[LOWER, b]
+        ratio = bins_ref[RATIO, b]
+        wind = jnp.maximum(bins_ref[COS, b] * gain_x[...] + bins_ref[SIN, b] * gain_y[...], 0.0)
         quad = quad_gain * (energy * (above + below) - 2.0 * above * below)
         grown = energy + energy * (ratio * (wind + quad))
         top = jnp.where(open_sea[...] > 0.0, grown, energy)
-        bottom = 1.0 + bins_ref[b, DAMP] * total[step] + ice[...]
+        bottom = 1.0 + bins_ref[DAMP, b] * total[step] + ice[...]
         wide[step, b, pl.ds(BASE, columns)] = jnp.where(flags[...] == 0, 0.0, top / bottom)
 
     def halves(values):
@@ -270,12 +281,12 @@
                 lon_taps[signs[i], rows_out], jnp.concatenate(pair_of, axis=0), preferred_element_type=jnp.float32
             )
             start, end = i * ext + rows_out.start, i * ext + rows_out.start + rows_out.size
-            east = (bins_ref[b, EAST] + bins_ref[b, WEST]) * rows_ref[...]
+            east = (bins_ref[EAST, b] + bins_ref[WEST, b]) * rows_ref[0:1]
             results.append(
                 field[rows_out.start : rows_out.start + rows_out.size]
                 + along_lon * east
-                + along_lat[start:end, :rows] * bins_ref[b, NORTH]
-                + along_lat[start:end, rows:] * bins_ref[b, SOUTH]
+                + along_lat[start:end, :rows] * bins_ref[NORTH, b]
+                + along_lat[start:end, rows:] * bins_ref[SOUTH, b]
             )
         return results
 
@@ -313,7 +324,8 @@
                     if b in mine and piece not in KEPT_BACK:
                         direct(step, piece).start()
 
-    inputs = [(field_hbm, first), (speed_hbm, speed), (heading_hbm, heading), (flags_hbm, flags)]
+    inputs = [(field_hbm, first), (speed_hbm, speed), (heading_hbm, heading), (flags_hbm, flags),
+              (bins_hbm.at[place], bins_ref), (rows_hbm, rows_ref)]
     inputs = [pltpu.make_async_copy(src, dst, in_sem.at[i]) for i, (src, dst) in enumerate(inputs)]
     for copy in inputs:
         copy.start()
@@ -328,11 +340,12 @@
     for sign, taps in enumerate((PLUS, MINUS)):
         lon_band, lat_band = band((ext, ext), 1, 0, taps), band((rows, rows), 0, 1, taps)
         lon_taps[sign] = jnp.concatenate([lon_band, lon_band], axis=1)
-        for half in range(2):
-            lat_taps[pl.ds(half * rows, rows), pl.ds(sign * rows, rows)] = lat_band
+        for part_of in range(2):
+            lat_taps[pl.ds(part_of * rows, rows), pl.ds(sign * rows, rows)] = lat_band
     for step in range(1, STEPS):
         part[step] = jnp.zeros((columns, rows), jnp.float32)
-    inputs[0].wait()
+    for copy in inputs[4:] + inputs[:1]:
+        copy.wait()
     part[0] = lax.fori_loop(0, here, lambda b, so_far: so_far + square(b, first[b]), jnp.zeros((columns, rows), jnp.float32))
     pl.semaphore_wait(barrier, len(partners))
 
@@ -341,18 +354,19 @@
         leg(0, piece).start()
     for piece in (3, 4, 5, 6, 0):
         direct(0, piece).start()
-    for copy in inputs[1:]:
+    for copy in inputs[1:4]:
         copy.wait()
     gain = wind_gain * 0.1 * speed[...]
     gain_x[...] = gain * jnp.cos(heading[...])
     gain_y[...] = gain * jnp.sin(heading[...])
     open_sea[...] = jnp.where(flags[...] == 1, 1.0, 0.0)
     ice[...] = jnp.where(flags[...] == 2, ice_loss, 0.0)
+    spread_z(0)
+    direct(0, 1).start()
     spread_b(0)
-    direct(0, 1).start()
+    direct(0, 2).start()
     pass_on_far(0, (0, 1, 2))
     spread_c(0)
-    direct(0, 2).start()
     pass_on_far(0, (3, 4))
     pass_on_shared(0)
     spread_end(0)
@@ -361,10 +375,12 @@
         if step > 0:
             spread_a(step)
             direct(step, 1).start()
-            pass_on_far(step, (1, 2))
+            pass_on_far(step, (1,))
+            spread_z(step)
+            direct(step, 2).start()
+            pass_on_far(step, (2, 3))
             spread_b(step)
-            direct(step, 2).start()
-            pass_on_far(step, (3, 4))
+            pass_on_far(step, (4,))
             pass_on_shared(step)
             spread_c(step)
             pass_on_far(step, (0,))
@@ -398,10 +414,12 @@
                     result_copy(group).start()
 
     for step in range(STEPS):
-        for turn in range(1, RING):
+        z_copy(step).wait_send()
+        for turn in range(1, ROW):
             a_copy(step, turn).wait_send()
+            c_copy(step, turn).wait_send()
+        for turn in range(1, LINES):
             b_copy(step, turn).wait_send()
-            c_copy(step, turn).wait_send()
         for piece in range(PIECES):
             arrival(step, piece).wait_send()
         for piece in range(len(FAR)):
@@ -419,9 +437,8 @@
 
 def shards(spectrum, wind_speed, wind_dir, flags):
     here, columns, rows = spectrum.shape
-    index = lax.axis_index("bins") * here + jnp.arange(here, dtype=jnp.int32)
     whole = (columns, rows)
-    chunk = columns // RING
+    chunk = columns // ROW
     ext = columns + 2 * BASE
     hbm = pl.BlockSpec(memory_space=pl.ANY)
     dma = pltpu.SemaphoreType.DMA
@@ -432,7 +449,7 @@
     return pl.pallas_call(
         kernel,
         out_shape=jax.ShapeDtypeStruct(spectrum.shape, jnp.float32),
-        in_specs=[hbm] * 4 + [pl.BlockSpec(memory_space=pltpu.SMEM), pl.BlockSpec(memory_space=pltpu.VMEM)],
+        in_specs=[hbm] * 6,
         out_specs=hbm,
         scratch_shapes=[
             buffer(here, *whole),
@@ -445,6 +462,8 @@
             buffer(GROUP, ext, rows),
             pltpu.VMEM((2, ext, 2 * ext), jnp.bfloat16),
             pltpu.VMEM((2 * rows, 2 * rows), jnp.bfloat16),
+            pltpu.SMEM((16, 128), jnp.float32),
+            buffer(8, rows),
             buffer(*whole),
             buffer(*whole),
             pltpu.VMEM(whole, jnp.int32),
@@ -453,20 +472,25 @@
             buffer(*whole),
             buffer(*whole),
             buffer(STEPS, *whole),
-            buffer(STEPS, RING, chunk, rows),
+            buffer(STEPS, ROW, chunk, rows),
             buffer(STEPS, chunk, rows),
-            buffer(STEPS, RING, chunk, rows),
+            buffer(STEPS, chunk, rows),
+            buffer(STEPS, chunk, rows),
+            buffer(STEPS, LINES, chunk, rows),
             buffer(STEPS, *whole),
         ]
         + [dma((STEPS, PIECES))] * 2
         + [dma((STEPS, len(FAR)))] * 2
         + [dma((STEPS, 2, GROUPS))] * 2
-        + [dma((STEPS, RING))] * 6
-        + [dma((4,)), dma((GROUPS,))],
+        + [dma((STEPS, ROW))] * 2
+        + [dma((STEPS,))] * 2
+        + [dma((STEPS, LINES))] * 2
+        + [dma((STEPS, ROW))] * 2
+        + [dma((6,)), dma((GROUPS,))],
         compiler_params=pltpu.CompilerParams(
             collective_id=0, has_side_effects=True, vmem_limit_bytes=56 * 1024 * 1024
         ),
-    )(spectrum, wind_speed, wind_dir, flags, bin_table(index), row_table(rows))
+    )(spectrum, wind_speed, wind_dir, flags, bin_table(lax.axis_size("bins"), here), row_table(rows))
 
 
 def solution(mesh):

time: 90.9 us -> 95.7 us (1.053)
  Pallas kernels: 86.8 us -> 93.3 us
    pallas_call x1, Pallas kernels: 86.8 us -> 93.3 us  [shards(): pl.pallas_call(kernel, out_shape=jax.ShapeDtypeStruct(spectrum.shape, jnp...]
where the time goes in v5:
time: 95.7 us; the launch traced here: 95.3 us
  Pallas kernels  93.3 us (97%)
  local copies, waits for them, and re-layouts  1.93 us (2%)
    pallas_call x1, Pallas kernels, shards(): pl.pallas_call(kernel, out_shape=jax.ShapeDtypeStruct(spectrum.shape, jnp...  93.3 us
    unnamed x1, local copies, waits for them, and re-layouts  1.93 us

profile of v5, /device:TPU:1, one launch (start us, length us, event | category | flops | bytes accessed | tf_op | source)
XLA Modules:
  0.0 95.3 jit_solution(6650879148440413485)
XLA Ops:
  0.0 93.3 %shard_map.64 = f32[18,64,128]{2,1,0:T(8,128)} custom-call(f32[18,64,128]{2,1,0:T(8,128)} %field_hbm.1, f32[64,128]{1,0:T(8,128)} %speed_hbm.1, f32[64,128]{1,0:T(8,128)} %heading_hbm.1, s32[64,128]{1,0:T(8,128)} %flags_hbm.1, f32[64,16,128]{2,1,0:T(8,128)} %constant.4.clone.bins_hbm, f32[8,128]{1,0:T(8,128)} %constant.5.clone.rows_hbm), custom_call_target="tpu_custom_call" | custom-call | tf_op jit(solution)/shard_map/pallas_call | solution.py:449
  93.3 1.9 %copy.8 = f32[18,64,128]{2,1,0:T(8,128)} copy(f32[18,64,128]{2,1,0:T(8,128)} %shard_map.64) | data formatting | bytes 1179648

commit v6 on v5

--- a/solution.py
+++ b/solution.py
@@ -34,7 +34,6 @@
 )
 SHARED = ((3, 12, 2, 0), (4, 14, 3, 2), (5, 17, 1, 5))
 FAR = ((0, 16, 2, 0, -1), (1, 0, 3, 8, 1), (1, 3, 3, 11, -1), (1, 6, 3, 14, 1), (1, 9, 1, 17, -1))
-KEPT_BACK = (1, 2)
 S0, F0 = len(DIRECT), len(DIRECT) + len(SHARED)
 PIECES = F0 + len(FAR)
 NEEDS = (
@@ -181,9 +180,9 @@
             leg(step, piece).wait_recv()
             second_leg(step, piece).start()
 
-    def pass_on_shared(step):
-        for piece, (before, *_) in enumerate(SHARED):
-            direct(step, before).wait_recv()
+    def pass_on_shared(step, pieces):
+        for piece in pieces:
+            direct(step, SHARED[piece][0]).wait_recv()
             shared(step, piece).start()
 
     def halo_copy(step, group, side):
@@ -321,7 +320,7 @@
                     if b in mine:
                         leg(step, piece).start()
                 for piece, (_, b, *_) in enumerate(DIRECT):
-                    if b in mine and piece not in KEPT_BACK:
+                    if b in mine:
                         direct(step, piece).start()
 
     inputs = [(field_hbm, first), (speed_hbm, speed), (heading_hbm, heading), (flags_hbm, flags),
@@ -352,7 +351,7 @@
     spread_a(0)
     for piece in range(len(FAR)):
         leg(0, piece).start()
-    for piece in (3, 4, 5, 6, 0):
+    for piece in (3, 4, 5, 0, 6, 1, 2):
         direct(0, piece).start()
     for copy in inputs[1:4]:
         copy.wait()
@@ -362,28 +361,23 @@
     open_sea[...] = jnp.where(flags[...] == 1, 1.0, 0.0)
     ice[...] = jnp.where(flags[...] == 2, ice_loss, 0.0)
     spread_z(0)
-    direct(0, 1).start()
+    pass_on_far(0, (0, 1))
+    pass_on_shared(0, (0, 1, 2))
     spread_b(0)
-    direct(0, 2).start()
-    pass_on_far(0, (0, 1, 2))
+    pass_on_far(0, (2, 3, 4))
     spread_c(0)
-    pass_on_far(0, (3, 4))
-    pass_on_shared(0)
     spread_end(0)
 
     for step in range(STEPS):
         if step > 0:
             spread_a(step)
-            direct(step, 1).start()
-            pass_on_far(step, (1,))
+            pass_on_far(step, (1, 2, 3))
             spread_z(step)
-            direct(step, 2).start()
-            pass_on_far(step, (2, 3))
+            pass_on_far(step, (4,))
+            pass_on_shared(step, (0, 1, 2))
+            pass_on_far(step, (0,))
             spread_b(step)
-            pass_on_far(step, (4,))
-            pass_on_shared(step)
             spread_c(step)
-            pass_on_far(step, (0,))
             spread_end(step)
 
         @pl.loop(0, GROUPS + LAG)

time: 95.7 us -> 94.4 us (0.986)
  Pallas kernels: 93.3 us -> 92.3 us
    pallas_call x1, Pallas kernels: 93.3 us -> 92.3 us  [shards(): pl.pallas_call(kernel, out_shape=jax.ShapeDtypeStruct(spectrum.shape, jnp...]
where the time goes in v6:
time: 94.4 us; the launch traced here: 94.2 us
  Pallas kernels  92.3 us (98%)
  local copies, waits for them, and re-layouts  1.93 us (2%)
    pallas_call x1, Pallas kernels, shards(): pl.pallas_call(kernel, out_shape=jax.ShapeDtypeStruct(spectrum.shape, jnp...  92.3 us
    unnamed x1, local copies, waits for them, and re-layouts  1.93 us

profile of v6, /device:TPU:1, one launch (start us, length us, event | category | flops | bytes accessed | tf_op | source)
XLA Modules:
  0.0 94.2 jit_solution(11293149479997619864)
XLA Ops:
  0.0 92.3 %shard_map.64 = f32[18,64,128]{2,1,0:T(8,128)} custom-call(f32[18,64,128]{2,1,0:T(8,128)} %field_hbm.1, f32[64,128]{1,0:T(8,128)} %speed_hbm.1, f32[64,128]{1,0:T(8,128)} %heading_hbm.1, s32[64,128]{1,0:T(8,128)} %flags_hbm.1, f32[64,16,128]{2,1,0:T(8,128)} %constant.4.clone.bins_hbm, f32[8,128]{1,0:T(8,128)} %constant.5.clone.rows_hbm), custom_call_target="tpu_custom_call" | custom-call | tf_op jit(solution)/shard_map/pallas_call | solution.py:443
  92.3 1.9 %copy.8 = f32[18,64,128]{2,1,0:T(8,128)} copy(f32[18,64,128]{2,1,0:T(8,128)} %shard_map.64) | data formatting | bytes 1179648

commit v7 on v2

--- a/solution.py
+++ b/solution.py
@@ -1,8 +1,8 @@
-import functools
 import math
 
 import jax
 import jax.numpy as jnp
+import numpy as np
 from jax import lax
 from jax.experimental import pallas as pl
 from jax.experimental.pallas import tpu as pltpu
@@ -46,41 +46,41 @@
 RATIO, COS, SIN, DAMP, UPPER, LOWER, EAST, WEST, NORTH, SOUTH = range(10)
 
 
-def bin_table(index):
-    direction = (index // NF).astype(jnp.float32)
-    level = (index % NF).astype(jnp.float32)
-    theta = direction * (2.0 * math.pi / ND)
-    ratio = jnp.power(1.05, level - NF // 2)
-    group = jnp.power(1.1, -level)
-    east = courant * group * jnp.cos(theta)
-    north = courant * group * jnp.sin(theta)
-    ratio, theta, east, north, level = (v[:, None] for v in (ratio, theta, east, north, level))
-    return jnp.concatenate(
-        [
-            ratio,
-            jnp.cos(theta),
-            jnp.sin(theta),
-            break_gain * ratio * ratio / (NF * ND),
-            (level + 2 < NF).astype(jnp.float32),
-            (level >= 2).astype(jnp.float32),
-            jnp.where(east >= 0.0, east / -60.0, 0.0),
-            jnp.where(east >= 0.0, 0.0, east / -60.0),
-            jnp.where(north >= 0.0, north / -60.0, 0.0),
-            jnp.where(north >= 0.0, 0.0, north / -60.0),
-        ],
-        axis=1,
+def bin_table(places, here):
+    index = np.arange(places * here).reshape(places, here)
+    theta = (index // NF).astype(np.float32) * np.float32(2.0 * math.pi / ND)
+    theta = theta.astype(np.float64)
+    level = index % NF
+    ratio = 1.05 ** (level - NF // 2.0)
+    east = courant * 1.1 ** (-level.astype(np.float64)) * np.cos(theta)
+    north = courant * 1.1 ** (-level.astype(np.float64)) * np.sin(theta)
+    table = np.zeros((places, 16, 128), np.float32)
+    values = (
+        ratio,
+        np.cos(theta),
+        np.sin(theta),
+        break_gain * ratio * ratio / (NF * ND),
+        level + 2 < NF,
+        level >= 2,
+        np.maximum(east, 0.0) / -60.0,
+        np.minimum(east, 0.0) / -60.0,
+        np.maximum(north, 0.0) / -60.0,
+        np.minimum(north, 0.0) / -60.0,
     )
+    for quantity, value in enumerate(values):
+        table[:, quantity, :here] = value
+    return table
 
 
 def row_table(rows):
-    lines = jnp.arange(rows).astype(jnp.float32)
-    coslat = jnp.cos((lines - rows / 2 + 0.5) * (0.25 * math.pi / 180.0))
-    return (1.0 / coslat).reshape(1, rows)
+    lines = np.arange(rows)
+    coslat = np.cos((lines - rows / 2 + 0.5) * (0.25 * math.pi / 180.0))
+    return np.broadcast_to(1.0 / coslat, (8, rows)).astype(np.float32)
 
 
 def kernel(
-    field_hbm, speed_hbm, heading_hbm, flags_hbm, bins_ref, rows_ref, out_ref,
-    first, later, last, got, relay, wide, one, two, lon_taps, lat_taps, speed, heading, flags, gain_x, gain_y, open_sea, ice,
+    field_hbm, speed_hbm, heading_hbm, flags_hbm, bins_hbm, rows_hbm, out_ref,
+    first, later, last, got, relay, wide, one, two, lon_taps, lat_taps, bins_ref, rows_ref, speed, heading, flags, gain_x, gain_y, open_sea, ice,
     part, part_in, mid, mid_in, total,
     send_sem, got_sem, leg_send, leg_recv, halo_send, halo_recv,
     a_send, a_recv, b_send, b_recv, c_send, c_recv, in_sem, out_sem,
@@ -211,7 +211,7 @@
         return send(theirs, theirs, c_send.at[step, turn], c_recv.at[step, turn], {"bins": in_row(turn)})
 
     def square(b, values):
-        scaled = bins_ref[b, RATIO] * values
+        scaled = bins_ref[RATIO, b] * values
         return scaled * scaled
 
     def spread_a(step):
@@ -244,14 +244,14 @@
 
     def source(step, b):
         energy = field_of(step)[b]
-        above = got[step, 0, b] * bins_ref[b, UPPER]
-        below = got[step, 1, b] * bins_ref[b, LOWER]
-        ratio = bins_ref[b, RATIO]
-        wind = jnp.maximum(bins_ref[b, COS] * gain_x[...] + bins_ref[b, SIN] * gain_y[...], 0.0)
+        above = got[step, 0, b] * bins_ref[UPPER, b]
+        below = got[step, 1, b] * bins_ref[LOWER, b]
+        ratio = bins_ref[RATIO, b]
+        wind = jnp.maximum(bins_ref[COS, b] * gain_x[...] + bins_ref[SIN, b] * gain_y[...], 0.0)
         quad = quad_gain * (energy * (above + below) - 2.0 * above * below)
         grown = energy + energy * (ratio * (wind + quad))
         top = jnp.where(open_sea[...] > 0.0, grown, energy)
-        bottom = 1.0 + bins_ref[b, DAMP] * total[step] + ice[...]
+        bottom = 1.0 + bins_ref[DAMP, b] * total[step] + ice[...]
         wide[step, b, pl.ds(BASE, columns)] = jnp.where(flags[...] == 0, 0.0, top / bottom)
 
     def halves(values):
@@ -270,12 +270,12 @@
                 lon_taps[signs[i], rows_out], jnp.concatenate(pair_of, axis=0), preferred_element_type=jnp.float32
             )
             start, end = i * ext + rows_out.start, i * ext + rows_out.start + rows_out.size
-            east = (bins_ref[b, EAST] + bins_ref[b, WEST]) * rows_ref[...]
+            east = (bins_ref[EAST, b] + bins_ref[WEST, b]) * rows_ref[0:1]
             results.append(
                 field[rows_out.start : rows_out.start + rows_out.size]
                 + along_lon * east
-                + along_lat[start:end, :rows] * bins_ref[b, NORTH]
-                + along_lat[start:end, rows:] * bins_ref[b, SOUTH]
+                + along_lat[start:end, :rows] * bins_ref[NORTH, b]
+                + along_lat[start:end, rows:] * bins_ref[SOUTH, b]
             )
         return results
 
@@ -313,7 +313,8 @@
                     if b in mine and piece not in KEPT_BACK:
                         direct(step, piece).start()
 
-    inputs = [(field_hbm, first), (speed_hbm, speed), (heading_hbm, heading), (flags_hbm, flags)]
+    inputs = [(field_hbm, first), (speed_hbm, speed), (heading_hbm, heading), (flags_hbm, flags),
+              (bins_hbm.at[place], bins_ref), (rows_hbm, rows_ref)]
     inputs = [pltpu.make_async_copy(src, dst, in_sem.at[i]) for i, (src, dst) in enumerate(inputs)]
     for copy in inputs:
         copy.start()
@@ -332,7 +333,8 @@
             lat_taps[pl.ds(half * rows, rows), pl.ds(sign * rows, rows)] = lat_band
     for step in range(1, STEPS):
         part[step] = jnp.zeros((columns, rows), jnp.float32)
-    inputs[0].wait()
+    for copy in inputs[4:] + inputs[:1]:
+        copy.wait()
     part[0] = lax.fori_loop(0, here, lambda b, so_far: so_far + square(b, first[b]), jnp.zeros((columns, rows), jnp.float32))
     pl.semaphore_wait(barrier, len(partners))
 
@@ -341,7 +343,7 @@
         leg(0, piece).start()
     for piece in (3, 4, 5, 6, 0):
         direct(0, piece).start()
-    for copy in inputs[1:]:
+    for copy in inputs[1:4]:
         copy.wait()
     gain = wind_gain * 0.1 * speed[...]
     gain_x[...] = gain * jnp.cos(heading[...])
@@ -419,7 +421,6 @@
 
 def shards(spectrum, wind_speed, wind_dir, flags):
     here, columns, rows = spectrum.shape
-    index = lax.axis_index("bins") * here + jnp.arange(here, dtype=jnp.int32)
     whole = (columns, rows)
     chunk = columns // RING
     ext = columns + 2 * BASE
@@ -432,7 +433,7 @@
     return pl.pallas_call(
         kernel,
         out_shape=jax.ShapeDtypeStruct(spectrum.shape, jnp.float32),
-        in_specs=[hbm] * 4 + [pl.BlockSpec(memory_space=pltpu.SMEM), pl.BlockSpec(memory_space=pltpu.VMEM)],
+        in_specs=[hbm] * 6,
         out_specs=hbm,
         scratch_shapes=[
             buffer(here, *whole),
@@ -445,6 +446,8 @@
             buffer(GROUP, ext, rows),
             pltpu.VMEM((2, ext, 2 * ext), jnp.bfloat16),
             pltpu.VMEM((2 * rows, 2 * rows), jnp.bfloat16),
+            pltpu.SMEM((16, 128), jnp.float32),
+            buffer(8, rows),
             buffer(*whole),
             buffer(*whole),
             pltpu.VMEM(whole, jnp.int32),
@@ -462,11 +465,11 @@
         + [dma((STEPS, len(FAR)))] * 2
         + [dma((STEPS, 2, GROUPS))] * 2
         + [dma((STEPS, RING))] * 6
-        + [dma((4,)), dma((GROUPS,))],
+        + [dma((6,)), dma((GROUPS,))],
         compiler_params=pltpu.CompilerParams(
             collective_id=0, has_side_effects=True, vmem_limit_bytes=56 * 1024 * 1024
         ),
-    )(spectrum, wind_speed, wind_dir, flags, bin_table(index), row_table(rows))
+    )(spectrum, wind_speed, wind_dir, flags, bin_table(lax.axis_size("bins"), here), row_table(rows))
 
 
 def solution(mesh):

time: 90.9 us -> 88.4 us (0.972)
  no operation moved by 1% of the time
where the time goes in v7:
time: 88.4 us; the launch traced here: 87.8 us
  Pallas kernels  85.9 us (97%)
  local copies, waits for them, and re-layouts  1.93 us (2%)
    pallas_call x1, Pallas kernels, shards(): pl.pallas_call(kernel, out_shape=jax.ShapeDtypeStruct(spectrum.shape, jnp...  85.9 us
    unnamed x1, local copies, waits for them, and re-layouts  1.93 us

profile of v7, /device:TPU:1, one launch (start us, length us, event | category | flops | bytes accessed | tf_op | source)
XLA Modules:
  0.0 87.8 jit_solution(5778818786213693774)
XLA Ops:
  0.0 85.9 %shard_map.64 = f32[18,64,128]{2,1,0:T(8,128)} custom-call(f32[18,64,128]{2,1,0:T(8,128)} %field_hbm.1, f32[64,128]{1,0:T(8,128)} %speed_hbm.1, f32[64,128]{1,0:T(8,128)} %heading_hbm.1, s32[64,128]{1,0:T(8,128)} %flags_hbm.1, f32[64,16,128]{2,1,0:T(8,128)} %constant.4.clone.bins_hbm, f32[8,128]{1,0:T(8,128)} %constant.5.clone.rows_hbm), custom_call_target="tpu_custom_call" | custom-call | tf_op jit(solution)/shard_map/pallas_call | solution.py:433
  85.9 1.9 %copy.8 = f32[18,64,128]{2,1,0:T(8,128)} copy(f32[18,64,128]{2,1,0:T(8,128)} %shard_map.64) | data formatting | bytes 1179648

commit v8 on v7

--- a/solution.py
+++ b/solution.py
@@ -34,7 +34,8 @@
 )
 SHARED = ((3, 12, 2, 0), (4, 14, 3, 2), (5, 17, 1, 5))
 FAR = ((0, 16, 2, 0, -1), (1, 0, 3, 8, 1), (1, 3, 3, 11, -1), (1, 6, 3, 14, 1), (1, 9, 1, 17, -1))
-KEPT_BACK = (1, 2)
+KEPT_BACK = (1, 2, 4, 5, 6)
+KEPT_FAR = (0,)
 S0, F0 = len(DIRECT), len(DIRECT) + len(SHARED)
 PIECES = F0 + len(FAR)
 NEEDS = (
@@ -307,7 +308,7 @@
             def _(k=k):
                 mine = range(k * GROUP, (k + 1) * GROUP)
                 for piece, (_, b, *_) in enumerate(FAR):
-                    if b in mine:
+                    if b in mine and piece not in KEPT_FAR:
                         leg(step, piece).start()
                 for piece, (_, b, *_) in enumerate(DIRECT):
                     if b in mine and piece not in KEPT_BACK:
@@ -341,8 +342,7 @@
     spread_a(0)
     for piece in range(len(FAR)):
         leg(0, piece).start()
-    for piece in (3, 4, 5, 6, 0):
-        direct(0, piece).start()
+    direct(0, 3).start()
     for copy in inputs[1:4]:
         copy.wait()
     gain = wind_gain * 0.1 * speed[...]
@@ -351,7 +351,8 @@
     open_sea[...] = jnp.where(flags[...] == 1, 1.0, 0.0)
     ice[...] = jnp.where(flags[...] == 2, ice_loss, 0.0)
     spread_b(0)
-    direct(0, 1).start()
+    for piece in (4, 5, 0, 6, 1):
+        direct(0, piece).start()
     pass_on_far(0, (0, 1, 2))
     spread_c(0)
     direct(0, 2).start()
@@ -362,7 +363,9 @@
     for step in range(STEPS):
         if step > 0:
             spread_a(step)
-            direct(step, 1).start()
+            leg(step, 0).start()
+            for piece in (4, 5, 6, 1):
+                direct(step, piece).start()
             pass_on_far(step, (1, 2))
             spread_b(step)
             direct(step, 2).start()

time: 88.4 us -> 87.7 us (level)
  the two profiles are of different devices: /device:TPU:1 before, /device:TPU:40 now
where the time goes in v8:
time: 87.7 us; the launch traced here: 87.5 us
  Pallas kernels  85.6 us (98%)
  local copies, waits for them, and re-layouts  1.93 us (2%)
    pallas_call x1, Pallas kernels, shards(): pl.pallas_call(kernel, out_shape=jax.ShapeDtypeStruct(spectrum.shape, jnp...  85.6 us
    unnamed x1, local copies, waits for them, and re-layouts  1.93 us

profile of v8, /device:TPU:40, one launch (start us, length us, event | category | flops | bytes accessed | tf_op | source)
XLA Modules:
  0.0 87.5 jit_solution(7294713502268021261)
XLA Ops:
  0.0 85.6 %shard_map.64 = f32[18,64,128]{2,1,0:T(8,128)} custom-call(f32[18,64,128]{2,1,0:T(8,128)} %field_hbm.1, f32[64,128]{1,0:T(8,128)} %speed_hbm.1, f32[64,128]{1,0:T(8,128)} %heading_hbm.1, s32[64,128]{1,0:T(8,128)} %flags_hbm.1, f32[64,16,128]{2,1,0:T(8,128)} %constant.4.clone.bins_hbm, f32[8,128]{1,0:T(8,128)} %constant.5.clone.rows_hbm), custom_call_target="tpu_custom_call" | custom-call | tf_op jit(solution)/shard_map/pallas_call | solution.py:436
  85.6 1.9 %copy.8 = f32[18,64,128]{2,1,0:T(8,128)} copy(f32[18,64,128]{2,1,0:T(8,128)} %shard_map.64) | data formatting | bytes 1179648

commit v9 on v8

--- a/solution.py
+++ b/solution.py
@@ -42,7 +42,6 @@
     ((F0, 0, S0, S0 + 1), (1, S0 + 2), (2, 6, F0 + 1), (F0 + 2,), (F0 + 3,), (F0 + 4,)),
     ((F0, S0), (0, 1, S0 + 1, S0 + 2), (2, 6, F0 + 1), (F0 + 2,), (F0 + 3,), (F0 + 4,)),
 )
-FIRST_GROUP = (0, 1)
 
 RATIO, COS, SIN, DAMP, UPPER, LOWER, EAST, WEST, NORTH, SOUTH = range(10)
 
@@ -280,16 +279,16 @@
             )
         return results
 
-    def advance(step, group):
-        bins = [group * GROUP + j for j in range(GROUP)]
+    def advance(step, groups_now):
+        bins = [group * GROUP + j for group in groups_now for j in range(GROUP)]
         directions = [(place * here + b) // NF for b in bins]
         signs = [(d + ND // 4) // (ND // 2) % 2 for d in directions]
         every, inner = pl.ds(0, ext), pl.ds(BASE, columns)
         for j, values in enumerate(rates([wide[step, b] for b in bins], bins, signs, every)):
             one[j] = values
-        for j, values in enumerate(rates([one[j] for j in range(GROUP)], bins, signs, every)):
+        for j, values in enumerate(rates([one[j] for j in range(len(bins))], bins, signs, every)):
             two[j] = 0.75 * wide[step, bins[j]] + 0.25 * values
-        for j, values in enumerate(rates([two[j] for j in range(GROUP)], bins, signs, inner)):
+        for j, values in enumerate(rates([two[j] for j in range(len(bins))], bins, signs, inner)):
             moved = wide[step, bins[j], inner] * (1.0 / 3.0) + (2.0 / 3.0) * values
             moved = jnp.where(flags[...] == 0, 0.0, moved)
             if step < STEPS - 1:
@@ -360,47 +359,64 @@
     pass_on_shared(0)
     spread_end(0)
 
-    for step in range(STEPS):
-        if step > 0:
-            spread_a(step)
-            leg(step, 0).start()
-            for piece in (4, 5, 6, 1):
-                direct(step, piece).start()
-            pass_on_far(step, (1, 2))
-            spread_b(step)
-            direct(step, 2).start()
-            pass_on_far(step, (3, 4))
-            pass_on_shared(step)
-            spread_c(step)
-            pass_on_far(step, (0,))
-            spread_end(step)
-
-        @pl.loop(0, GROUPS + LAG)
-        def _(g, step=step):
-            @pl.when(g < GROUPS)
-            def _():
-                group = (g + FIRST_GROUP[step]) % GROUPS
-                for k in range(GROUPS):
-                    @pl.when(group == k)
-                    def _(k=k):
-                        for piece in NEEDS[step][k]:
-                            arrival(step, piece).wait_recv()
-
-                for j in range(GROUP):
-                    source(step, group * GROUP + j)
-                for side in range(2):
-                    halo_copy(step, group, side).start()
-
-            @pl.when(g >= LAG)
-            def _():
-                group = (g - LAG + FIRST_GROUP[step]) % GROUPS
-                for side in range(2):
-                    halo_copy(step, group, side).wait_recv()
-                advance(step, group)
-                if step < STEPS - 1:
-                    send_group(step + 1, group)
-                else:
-                    result_copy(group).start()
+    def source_group(step, group):
+        for k in range(GROUPS):
+            @pl.when(group == k)
+            def _(k=k):
+                for piece in NEEDS[step][k]:
+                    arrival(step, piece).wait_recv()
+
+        for j in range(GROUP):
+            source(step, group * GROUP + j)
+        for side in range(2):
+            halo_copy(step, group, side).start()
+
+    def halos_there(step, group):
+        for side in range(2):
+            halo_copy(step, group, side).wait_recv()
+
+    @pl.loop(0, GROUPS + LAG)
+    def _(g):
+        @pl.when(g >= LAG)
+        def _():
+            group = g - LAG
+            halos_there(0, group)
+            advance(0, (group,))
+            send_group(1, group)
+
+        @pl.when(g < GROUPS)
+        def _():
+            source_group(0, g)
+
+    spread_a(1)
+    leg(1, 0).start()
+    for piece in (4, 5, 6, 1):
+        direct(1, piece).start()
+    pass_on_far(1, (1, 2))
+    spread_b(1)
+    direct(1, 2).start()
+    pass_on_far(1, (3, 4))
+    pass_on_shared(1)
+    spread_c(1)
+    pass_on_far(1, (0,))
+    spread_end(1)
+
+
+    @pl.loop(0, GROUPS // 2 + 1)
+    def _(g):
+        @pl.when(g < GROUPS // 2)
+        def _():
+            for j in range(2):
+                source_group(1, (2 * g + j + 1) % GROUPS)
+
+        @pl.when(g >= 1)
+        def _():
+            pair_now = [(2 * g + j - 1) % GROUPS for j in range(2)]
+            for group in pair_now:
+                halos_there(1, group)
+            advance(1, pair_now)
+            for group in pair_now:
+                result_copy(group).start()
 
     for step in range(STEPS):
         for turn in range(1, RING):
@@ -445,8 +461,8 @@
             buffer(STEPS, 2, here, *whole),
             buffer(STEPS, here, *whole),
             buffer(STEPS, here, ext, rows),
-            buffer(GROUP, ext, rows),
-            buffer(GROUP, ext, rows),
+            buffer(2 * GROUP, ext, rows),
+            buffer(2 * GROUP, ext, rows),
             pltpu.VMEM((2, ext, 2 * ext), jnp.bfloat16),
             pltpu.VMEM((2 * rows, 2 * rows), jnp.bfloat16),
             pltpu.SMEM((16, 128), jnp.float32),

time: 87.7 us -> 85.7 us (0.977)
  the two profiles are of different devices: /device:TPU:40 before, /device:TPU:1 now
where the time goes in v9:
time: 85.7 us; the launch traced here: 85.5 us
  Pallas kernels  83.6 us (98%)
  local copies, waits for them, and re-layouts  1.93 us (2%)
    pallas_call x1, Pallas kernels, shards(): pl.pallas_call(kernel, out_shape=jax.ShapeDtypeStruct(spectrum.shape, jnp...  83.6 us
    unnamed x1, local copies, waits for them, and re-layouts  1.93 us

profile of v9, /device:TPU:1, one launch (start us, length us, event | category | flops | bytes accessed | tf_op | source)
XLA Modules:
  0.0 85.5 jit_solution(17741999194350188999)
XLA Ops:
  0.0 83.6 %shard_map.64 = f32[18,64,128]{2,1,0:T(8,128)} custom-call(f32[18,64,128]{2,1,0:T(8,128)} %field_hbm.1, f32[64,128]{1,0:T(8,128)} %speed_hbm.1, f32[64,128]{1,0:T(8,128)} %heading_hbm.1, s32[64,128]{1,0:T(8,128)} %flags_hbm.1, f32[64,16,128]{2,1,0:T(8,128)} %constant.4.clone.bins_hbm, f32[8,128]{1,0:T(8,128)} %constant.5.clone.rows_hbm), custom_call_target="tpu_custom_call" | custom-call | tf_op jit(solution)/shard_map/pallas_call | solution.py:452
  83.6 1.9 %copy.8 = f32[18,64,128]{2,1,0:T(8,128)} copy(f32[18,64,128]{2,1,0:T(8,128)} %shard_map.64) | data formatting | bytes 1179648

commit v10 on v9

--- a/solution.py
+++ b/solution.py
@@ -350,13 +350,14 @@
     open_sea[...] = jnp.where(flags[...] == 1, 1.0, 0.0)
     ice[...] = jnp.where(flags[...] == 2, ice_loss, 0.0)
     spread_b(0)
-    for piece in (4, 5, 0, 6, 1):
+    for piece in (4, 5, 0, 6):
         direct(0, piece).start()
     pass_on_far(0, (0, 1, 2))
     spread_c(0)
-    direct(0, 2).start()
+    direct(0, 1).start()
     pass_on_far(0, (3, 4))
     pass_on_shared(0)
+    direct(0, 2).start()
     spread_end(0)
 
     def source_group(step, group):
@@ -390,14 +391,15 @@
 
     spread_a(1)
     leg(1, 0).start()
-    for piece in (4, 5, 6, 1):
+    for piece in (4, 5, 6):
         direct(1, piece).start()
     pass_on_far(1, (1, 2))
     spread_b(1)
-    direct(1, 2).start()
     pass_on_far(1, (3, 4))
     pass_on_shared(1)
     spread_c(1)
+    for piece in (1, 2):
+        direct(1, piece).start()
     pass_on_far(1, (0,))
     spread_end(1)
 

time: 85.7 us -> 86.7 us (1.012)
  Pallas kernels: 83.6 us -> 84.6 us
    pallas_call x1, Pallas kernels: 83.6 us -> 84.6 us  [shards(): pl.pallas_call(kernel, out_shape=jax.ShapeDtypeStruct(spectrum.shape, jnp...]
where the time goes in v10:
time: 86.7 us; the launch traced here: 86.6 us
  Pallas kernels  84.6 us (98%)
  local copies, waits for them, and re-layouts  1.93 us (2%)
    pallas_call x1, Pallas kernels, shards(): pl.pallas_call(kernel, out_shape=jax.ShapeDtypeStruct(spectrum.shape, jnp...  84.6 us
    unnamed x1, local copies, waits for them, and re-layouts  1.93 us

profile of v10, /device:TPU:1, one launch (start us, length us, event | category | flops | bytes accessed | tf_op | source)
XLA Modules:
  0.0 86.6 jit_solution(352331787216844335)
XLA Ops:
  0.0 84.6 %shard_map.64 = f32[18,64,128]{2,1,0:T(8,128)} custom-call(f32[18,64,128]{2,1,0:T(8,128)} %field_hbm.1, f32[64,128]{1,0:T(8,128)} %speed_hbm.1, f32[64,128]{1,0:T(8,128)} %heading_hbm.1, s32[64,128]{1,0:T(8,128)} %flags_hbm.1, f32[64,16,128]{2,1,0:T(8,128)} %constant.4.clone.bins_hbm, f32[8,128]{1,0:T(8,128)} %constant.5.clone.rows_hbm), custom_call_target="tpu_custom_call" | custom-call | tf_op jit(solution)/shard_map/pallas_call | solution.py:454
  84.6 1.9 %copy.8 = f32[18,64,128]{2,1,0:T(8,128)} copy(f32[18,64,128]{2,1,0:T(8,128)} %shard_map.64) | data formatting | bytes 1179648

commit v11 on v9

--- a/solution.py
+++ b/solution.py
@@ -35,6 +35,7 @@
 SHARED = ((3, 12, 2, 0), (4, 14, 3, 2), (5, 17, 1, 5))
 FAR = ((0, 16, 2, 0, -1), (1, 0, 3, 8, 1), (1, 3, 3, 11, -1), (1, 6, 3, 14, 1), (1, 9, 1, 17, -1))
 KEPT_BACK = (1, 2, 4, 5, 6)
+LATE_X = 3
 KEPT_FAR = (0,)
 S0, F0 = len(DIRECT), len(DIRECT) + len(SHARED)
 PIECES = F0 + len(FAR)
@@ -150,7 +151,7 @@
 
     def leg(step, piece):
         kind, b, bins, _, way = FAR[piece]
-        offset = 1 + 2 * far if kind else far - 1
+        offset = (1 + 2 * far if piece < LATE_X else 1 - far) if kind else far - 1
         return send(
             source_of(step).at[pl.ds(b, bins)], relay.at[step, pl.ds(b, bins)],
             leg_send.at[step, piece], leg_recv.at[step, piece], at(offset, way * LEG),
@@ -159,9 +160,10 @@
     def second_leg(step, piece):
         kind, b, bins, slot, way = FAR[piece]
         source_far = (height - way * LEG + around_z) % around_z // (sectors // 2)
+        offset = (1 - source_far if piece < LATE_X else 1 + 2 * source_far) if kind else 0
         return send(
             relay.at[step, pl.ds(b, bins)], got.at[step, kind, pl.ds(slot, bins)],
-            send_sem.at[step, F0 + piece], got_sem.at[step, F0 + piece], at(1 - source_far if kind else 0, way * LEG),
+            send_sem.at[step, F0 + piece], got_sem.at[step, F0 + piece], at(offset, way * LEG),
         )
 
     def arrival(step, piece):

time: 85.7 us -> 85.8 us (level)
  no operation moved by 1% of the time
where the time goes in v11:
time: 85.8 us; the launch traced here: 85.4 us
  Pallas kernels  83.4 us (97%)
  local copies, waits for them, and re-layouts  1.93 us (2%)
    pallas_call x1, Pallas kernels, shards(): pl.pallas_call(kernel, out_shape=jax.ShapeDtypeStruct(spectrum.shape, jnp...  83.4 us
    unnamed x1, local copies, waits for them, and re-layouts  1.93 us

profile of v11, /device:TPU:1, one launch (start us, length us, event | category | flops | bytes accessed | tf_op | source)
XLA Modules:
  0.0 85.4 jit_solution(9998129566613682987)
XLA Ops:
  0.0 83.4 %shard_map.64 = f32[18,64,128]{2,1,0:T(8,128)} custom-call(f32[18,64,128]{2,1,0:T(8,128)} %field_hbm.1, f32[64,128]{1,0:T(8,128)} %speed_hbm.1, f32[64,128]{1,0:T(8,128)} %heading_hbm.1, s32[64,128]{1,0:T(8,128)} %flags_hbm.1, f32[64,16,128]{2,1,0:T(8,128)} %constant.4.clone.bins_hbm, f32[8,128]{1,0:T(8,128)} %constant.5.clone.rows_hbm), custom_call_target="tpu_custom_call" | custom-call | tf_op jit(solution)/shard_map/pallas_call | solution.py:454
  83.5 1.9 %copy.8 = f32[18,64,128]{2,1,0:T(8,128)} copy(f32[18,64,128]{2,1,0:T(8,128)} %shard_map.64) | data formatting | bytes 1179648
